TPU v7x, 32 devices: a whole 2x2x4 slice. The times are simulated.
32 devices in a mesh: band: 4 (over y, x), fft: 8 (over z, core).
Axes of the slice: x: 2, y: 2, z: 4, core: 2. Of those that a mesh axis runs over, the one named last changes fastest.
Arguments:
- orbitals: float32 [2, 4, 144, 2048], P(None, 'band', None, 'fft'), may hold values from -27 to 27
- potential: float32 [288, 20736], P('fft'), may hold values from -3 to 1
- projectors: float32 [2, 16, 144, 2048], P(None, None, None, 'fft'), may hold values from -6 to 6
- coupling: float32 [16, 16], replicated, may hold values from -15 to 15
- stick_column: int32 [2048], replicated, may hold values from 0 to 20735, as said below
- stick_heights: int32 [144, 2048], P(None, 'fft'), may hold values from 0 to 287, as said below
- projector_atom: int32 [16], replicated, may hold values from 0 to 3, never falling along the last dimension, each value on 1 to 8 neighbouring positions
Outputs:
- applied_h: float32 [2, 4, 144, 2048], P(None, 'band', None, 'fft')
- projections: float32 [2, 16, 4], P(None, None, 'band')
- subspace: float32 [2, 4, 4], replicated
Inputs may be any that keep to these rules, and one draw needn't show every extreme that they name: `stick_column`: the sticks name distinct grid points; points 0 and 20735 are always among them. `stick_heights`: the 144 slots of each stick name distinct heights. `projector_atom`: never falls along the projectors; every atom has 1 to 8 projectors.
All inputs are finite; a program needn't handle non-finite values.
Results may differ from a plain program's by a relative error of at most 0.000073.
Values sent between devices are 32-bit elements; how exact they have to be, the bound alone decides.
A program may use at most 192 MiB of HBM per device.

v0:
```python
import math

import jax
import jax.numpy as jnp
from jax import lax
from jax.sharding import PartitionSpec as P

NX = 144
NY = 144
NZ = 288


KINETIC = 8.0
HIGHEST = lax.Precision.HIGHEST


def frequency(position, length):
    return jnp.where(position < (length + 1) // 2, position, position - length).astype(jnp.float32)


def dft_table(length, sign):
    points = jnp.arange(length, dtype=jnp.int32)
    phase = points[:, None] * points[None, :] % length
    angle = 2.0 * math.pi / length * phase.astype(jnp.float32)
    cosine = jnp.cos(angle)
    sine = sign * jnp.sin(angle)
    return jnp.stack([jnp.stack([cosine, -sine], 1), jnp.stack([sine, cosine], 1)], 0)


def conj_pairs(left, right):
    blocks = jnp.einsum("pmgs,qngs->pqmn", left, right, precision=HIGHEST)
    return jnp.stack([blocks[0, 0] + blocks[1, 1], blocks[0, 1] - blocks[1, 0]], 0)


def reduce_planes(block):
    return lax.psum(block, "fft")


def body(orbitals, potential, projectors, coupling, stick_column, stick_heights, projector_atom):
    bands_here = orbitals.shape[1]
    slot_count = orbitals.shape[2]
    sticks_here = orbitals.shape[3]
    planes_here = potential.shape[0]
    stick_total = stick_column.shape[0]
    coeff_total = slot_count * stick_total
    grid_total = NX * NY * NZ
    all_orbitals = lax.all_gather(orbitals, "band", axis=1, tiled=True)
    first_stick = lax.axis_index("fft") * sticks_here
    local_columns = lax.dynamic_slice_in_dim(stick_column, first_stick, sticks_here)
    along_x = frequency(local_columns // NY, NX) / NX
    along_y = frequency(local_columns % NY, NY) / NY
    along_z = frequency(stick_heights, NZ) / NZ
    kinetic = (
        KINETIC * (along_x * along_x + along_y * along_y)[None, :] + KINETIC * along_z * along_z
    )
    stick_slots = jnp.broadcast_to(
        jnp.arange(sticks_here, dtype=jnp.int32)[None, :], stick_heights.shape
    )
    column_zero = jnp.zeros((2, bands_here, NZ, sticks_here), jnp.float32)
    columns_dense = column_zero.at[:, :, stick_heights, stick_slots].set(orbitals)
    z_space = jnp.einsum("pzqk,qbks->pbzs", dft_table(NZ, 1.0), columns_dense, precision=HIGHEST)
    table_x_in = dft_table(NX, 1.0)
    table_y_in = dft_table(NY, 1.0)
    table_x_out = dft_table(NX, -1.0)
    table_y_out = dft_table(NY, -1.0)
    potential_grid = potential.reshape(planes_here, NX, NY)
    planes = lax.all_to_all(z_space, "fft", split_axis=2, concat_axis=3, tiled=True)
    band_count = planes.shape[1]
    flat = (
        jnp.zeros((2, band_count, planes_here, NX * NY), jnp.float32)
        .at[:, :, :, stick_column]
        .set(planes)
    )
    spatial = flat.reshape(2, band_count, planes_here, NX, NY)
    spatial = jnp.einsum("pyqv,qbzxv->pbzxy", table_y_in, spatial, precision=HIGHEST)
    spatial = jnp.einsum("pxqu,qbzuy->pbzxy", table_x_in, spatial, precision=HIGHEST)
    spatial = spatial * potential_grid[None, None]
    spatial = jnp.einsum("pxqu,qbzuy->pbzxy", table_x_out, spatial, precision=HIGHEST)
    spatial = jnp.einsum("pyqv,qbzxv->pbzxy", table_y_out, spatial, precision=HIGHEST)
    results = lax.all_to_all(
        spatial.reshape(2, band_count, planes_here, NX * NY)[:, :, :, stick_column],
        "fft",
        split_axis=3,
        concat_axis=2,
        tiled=True,
    )
    freq_space = jnp.einsum("pzqk,qbks->pbzs", dft_table(NZ, -1.0), results, precision=HIGHEST)
    local_term = freq_space[:, :, stick_heights, stick_slots] / grid_total
    norm_scale = 1.0 / math.sqrt(coeff_total)
    raw_products = jnp.einsum("pkgs,qbgs->pqkb", projectors, orbitals, precision=HIGHEST)
    partial_proj = jnp.stack(
        [raw_products[0, 0] + raw_products[1, 1], raw_products[0, 1] - raw_products[1, 0]], 0
    )
    projections = lax.psum(partial_proj, "fft") * norm_scale
    same_atom = projector_atom[:, None] == projector_atom[None, :]
    atom_coupling = jnp.where(same_atom, 0.5 * (coupling + coupling.T), jnp.zeros_like(coupling))
    weighted = jnp.einsum("kl,plb->pkb", atom_coupling, projections, precision=HIGHEST)
    spread = jnp.einsum("pkgs,qkb->pqbgs", projectors, weighted, precision=HIGHEST)
    nonlocal_term = (
        jnp.stack([spread[0, 0] - spread[1, 1], spread[0, 1] + spread[1, 0]], 0) * norm_scale
    )
    applied_h = kinetic * orbitals + local_term + nonlocal_term
    block = conj_pairs(all_orbitals, applied_h)
    summed = reduce_planes(block) / coeff_total
    subspace = lax.all_gather(summed, "band", axis=2, tiled=True)
    return (applied_h, projections, subspace)


def solution(mesh):
    in_specs = (
        P(None, "band", None, "fft"),
        P("fft", None),
        P(None, None, None, "fft"),
        P(),
        P(),
        P(None, "fft"),
        P(),
    )
    out_specs = (P(None, "band", None, "fft"), P(None, None, "band"), P())
    return jax.shard_map(body, mesh=mesh, in_specs=in_specs, out_specs=out_specs, check_vma=False)
```

profile of v0, /device:TPU:0, one launch (start us, length us, event | category | flops | bytes accessed | tf_op | source)
XLA Modules:
  0.0 1313.7 jit_solution(15797394559530293460)
XLA Ops:
  15.7 10.4 copy.159
  26.1 105.4 %scatter_custom_fusion.1 = f32[2,73728]{0,1:T(8,128)} fusion(s32[36864]{0:T(1024)S(1)} %bitcast.222, f32[36864,2]{1,0:T(8,128)} %bitcast.210, f32[]{:T(128)} %constant.98.clone.1), kind=kCustom, calls=%fused_computation.4 | custom fusion | bytes 590336
  131.5 21.3 %copy.117 = f32[2,288,256]{2,1,0:T(8,128)S(1)} copy(f32[2,288,256]{0,2,1:T(8,128)} %bitcast.205) | data formatting | bytes 1179648 | tf_op jit(solution)/shard_map/reshape.1
  158.0 6.5 all-to-all-start
  166.2 6.4 mul.391
  172.5 6.6 copy.123
  179.3 18.3 %fusion.32 = f32[2,2,16]{2,0,1:T(2,128)S(1)} fusion(f32[2,16,144,256]{3,2,1,0:T(8,128)} %param.9, f32[2,144,256]{2,1,0:T(8,128)S(1)} %bitcast.214), kind=kOutput, calls=%fused_computation.32 | convolution fusion | flops 28311552 | bytes 5013760 | tf_op jit(solution)/shard_map/pkgs,qbgs->pqkb/dot_general | solution.py:90
  197.6 17.6 %psum.14 = f32[2,16,1]{1,2,0:T(1,128)S(1)} all-reduce(f32[2,16,1]{1,2,0:T(1,128)S(1)} %pad_maximum_fusion.8), channel_id=1, replica_groups=mesh['band'=4,'fft'=8] {'fft'}, use_global_device_ids=true, to_apply=%region_2.3 | all-reduce | flops 32 | bytes 256 | tf_op jit(solution)/shard_map/psum | solution.py:94
  219.9 2.6 copy.120
  222.5 7.4 broadcast.419
  229.9 186.7 %scatter_fusion = f32[2,36,20736]{1,0,2:T(2,128)} fusion(f32[2,36,20736]{1,0,2:T(2,128)} %broadcast.419, s32[2048]{0:T(1024)S(1)} %get-tuple-element.27, f32[2048,2,36]{2,1,0:T(2,128)S(1)} %copy.120), kind=kCustom, calls=%fused_computation.2 | custom fusion | bytes 1777664 | tf_op jit(solution)/shard_map/scatter | solution.py:72
  416.6 33.1 %copy.147 = f32[2,36,144,144,1]{3,2,0,4,1:T(8,128)} copy(f32[2,36,144,144,1]{1,0,3,2,4:T(2,128)} %bitcast.206) | data formatting | bytes 11943936 | tf_op jit(solution)/shard_map/reshape.5
  449.7 20.8 %fusion.45 = f32[36,144,2,144,1]{3,1,4,2,0:T(8,128)S(1)} fusion(f32[2,36,144,144,1]{3,2,0,4,1:T(8,128)} %copy.147, f32[1,144,2,144]{3,1,2,0:T(8,128)S(1)} %copy-done.3, f32[1,144,2,144]{3,1,2,0:T(8,128)S(1)} %copy-done.4), kind=kOutput, calls=%fused_computation.49 | convolution fusion | flops 5159863296 | bytes 12275712 | tf_op jit(solution)/shard_map/pyqv,qbzxv->pbzxy/dot_general | solution.py:75
  470.6 48.3 %fusion.4 = f32[36,144,2,144,1]{3,1,4,2,0:T(8,128)S(1)} fusion(f32[36,144,2,144,1]{3,1,4,2,0:T(8,128)S(1)} %fusion.45, f32[1,144,2,144]{3,1,2,0:T(8,128)S(1)} %copy-done.3, f32[1,144,2,144]{3,1,2,0:T(8,128)S(1)} %copy-done.4), kind=kOutput, calls=%fused_computation.8 | convolution fusion | flops 5159863296 | bytes 12275712 | tf_op jit(solution)/shard_map/pxqu,qbzuy->pbzxy/dot_general | solution.py:76
  518.9 19.2 %fusion.6 = f32[36,144,2,144,1]{3,1,4,2,0:T(8,128)S(1)} fusion(f32[36,144,2,144,1]{3,1,4,2,0:T(8,128)S(1)} %fusion.4, f32[36,144,144]{1,2,0:T(8,128)S(1)} %bitcast.209, f32[1,144,2,144]{3,1,2,0:T(8,128)S(1)} %copy-done.2, f32[1,144,2,144]{3,1,2,0:T(8,128)S(1)} %copy-done.1), kind=kOutput, calls=%fused_computation.10 | convolution fusion | flops 5161356288 | bytes 15261696 | tf_op jit(solution)/shard_map/pxqu,qbzuy->pbzxy/dot_general | solution.py:78
  538.0 59.7 %fusion.13 = f32[2,1,36,144,144]{4,3,0,2,1:T(8,128)} fusion(f32[36,144,2,144,1]{3,1,4,2,0:T(8,128)S(1)} %fusion.6, f32[1,144,2,144]{3,1,2,0:T(8,128)S(1)} %copy-done.2, f32[1,144,2,144]{3,1,2,0:T(8,128)S(1)} %copy-done.1), kind=kOutput, calls=%fused_computation.19 | convolution fusion | flops 5159863296 | bytes 12275712 | tf_op jit(solution)/shard_map/pyqv,qbzxv->pbzxy/dot_general | solution.py:79
  597.7 29.2 %copy.166 = f32[2,1,36,144,144]{2,0,4,3,1:T(2,128)} copy(f32[2,1,36,144,144]{4,3,0,2,1:T(8,128)} %fusion.13) | data formatting | bytes 11943936 | tf_op jit(solution)/shard_map/reshape | solution.py:81
  626.9 21.5 %gather_fusion = f32[2048,2,36]{2,1,0:T(2,128)} fusion(f32[2,36,20736]{1,0,2:T(2,128)} %bitcast.207, s32[2048]{0:T(1024)S(1)} %get-tuple-element.26), kind=kCustom, calls=%fused_computation | custom fusion | bytes 1187840 | tf_op jit(solution)/shard_map/gather | solution.py:81
  650.0 4.9 reshape.509
  655.0 3.7 all-to-all-start.1
  660.3 7.2 fusion.9
  669.2 6.1 all-to-all-done.1
  675.9 3.0 reduce.4
  678.9 4.8 reshape.510
  685.7 3.0 fusion.24
  688.7 18.6 %copy.129 = f32[2,288,256]{0,2,1:T(8,128)} copy(f32[2,288,256]{2,1,0:T(8,128)S(1)} %fusion.24) | data formatting | bytes 1179648 | tf_op jit(solution)/shard_map/pzqk,qbks->pbzs/transpose | solution.py:87
  707.2 532.5 %gather_fusion.1 = f32[36864,2]{1,0:T(8,128)} fusion(f32[2,288,256]{0,2,1:T(8,128)} %copy.129, s32[36864]{0:T(1024)S(1)} %bitcast.204), kind=kCustom, calls=%fused_computation.1 | custom fusion | bytes 884736 | tf_op jit(solution)/shard_map/gather | solution.py:88
  1239.7 14.7 %broadcast_multiply_fusion = f32[36864,2]{1,0:T(8,128)} fusion(f32[36864,2]{1,0:T(8,128)} %gather_fusion.1), kind=kLoop, calls=%fused_computation.13 | loop fusion | flops 73728 | bytes 589824 | tf_op jit(solution)/shard_map/div | solution.py:88
  1254.4 10.6 copy.171
  1265.8 16.8 %fusion.35 = f32[2,2,4]{2,0,1:T(2,128)S(1)} fusion(f32[2,4,144,256]{3,2,0,1:T(8,128)} %all-gather.2.cloned.1.call-done, f32[2,1,144,256]{3,1,2,0:T(1,128)S(1)} %fusion.57), kind=kOutput, calls=%fused_computation.33 | convolution fusion | flops 7077888 | bytes 1474624 | tf_op jit(solution)/shard_map/pmgs,qngs->pqmn/dot_general | solution.py:31
  1282.7 14.5 %psum.15 = f32[2,4,1]{1,0,2:T(2,128)S(1)} all-reduce(f32[2,4,1]{1,0,2:T(2,128)S(1)} %pad_maximum_fusion.9), channel_id=1, replica_groups=mesh['band'=4,'fft'=8] {'fft'}, use_global_device_ids=true, to_apply=%region_3.4 | all-reduce | flops 8 | bytes 64 | tf_op jit(solution)/shard_map/psum | solution.py:36
  1297.9 8.1 all_gather.7
  (75 shorter events, 29.9 us)
Async XLA Ops:
  158.0 21.3 %copy-start = (f32[2,1,144,256]{3,2,1,0:T(8,128)S(1)}, f32[2,1,144,256]{3,2,1,0:T(8,128)}, u32[]{:S(2)}) copy-start(f32[2,1,144,256]{3,2,1,0:T(8,128)} %param.7) | copy-start | bytes 884740
  158.0 60.5 %all-to-all-start = ((f32[2,1,288,256]{3,0,1,2:T(2,128)}), f32[2,1,288,256]{3,0,1,2:T(2,128)S(1)}, u32[]{:S(2)}, u32[]{:S(2)}) async-start(f32[2,1,288,256]{3,0,1,2:T(2,128)} %copy.118), calls=%async_computation | async-start | bytes 1179648 | tf_op jit(solution)/shard_map/all_to_all | solution.py:67
  164.4 1101.4 %all-gather.2.cloned.1.call-start = ((), (), s32[]{:S(2)}) async-start(), calls=%async_computation.2 | async-start | bytes 1474560 | tf_op jit(solution)/shard_map/all_gather | solution.py:47
  166.1 49.1 %copy-start.9 = (f32[16,16]{1,0:T(8,128)S(1)}, f32[16,16]{1,0:T(8,128)}, u32[]{:S(2)}) copy-start(f32[16,16]{1,0:T(8,128)} %param.10) | copy-start | bytes 3076
  166.1 49.2 %copy-start.8 = (s32[2048]{0:T(1024)S(1)}, s32[2048]{0:T(1024)}, u32[]{:S(2)}) copy-start(s32[2048]{0:T(1024)} %param.11) | copy-start | bytes 24580
  166.2 49.3 %copy-start.11 = (s32[16]{0:T(128)S(1)}, s32[16]{0:T(128)}, u32[]{:S(2)}) copy-start(s32[16]{0:T(128)} %param.13) | copy-start | bytes 196
  215.4 14.5 %copy-start.10 = (f32[2,16,1]{1,2,0:T(1,128)}, f32[2,16,1]{1,2,0:T(1,128)S(1)}, u32[]{:S(2)}) copy-start(f32[2,16,1]{1,2,0:T(1,128)S(1)} %broadcast_multiply_fusion.4) | copy-start | bytes 388
  416.6 33.1 %copy-start.3 = (f32[1,144,2,144]{3,1,2,0:T(8,128)S(1)}, f32[1,144,2,144]{3,1,2,0:T(8,128)}, u32[]{:S(2)}) copy-start(f32[1,144,2,144]{3,1,2,0:T(8,128)} %get-tuple-element.24) | copy-start | bytes 497668
  416.6 33.1 %copy-start.4 = (f32[1,144,2,144]{3,1,2,0:T(8,128)S(1)}, f32[1,144,2,144]{3,1,2,0:T(8,128)}, u32[]{:S(2)}) copy-start(f32[1,144,2,144]{3,1,2,0:T(8,128)} %get-tuple-element.25) | copy-start | bytes 497668
  449.7 69.1 %slice-start = ((s8[5308416]{0:T(1024)(128)(4,1)}), s8[4194304]{0:T(1024)(128)(4,1)S(1)}, s32[]{:S(2)}) async-start(s8[5308416]{0:T(1024)(128)(4,1)} %bitcast.208), calls=%async_computation.3 | async-start | bytes 8388608
  470.5 48.3 %slice-start.1 = ((s8[5308416]{0:T(1024)(128)(4,1)}), s8[1114112]{0:T(1024)(128)(4,1)S(1)}, s32[]{:S(2)}) async-start(s8[5308416]{0:T(1024)(128)(4,1)} %bitcast.208), calls=%async_computation.4 | async-start | bytes 2228224
  470.5 48.3 %copy-start.1 = (f32[1,144,2,144]{3,1,2,0:T(8,128)S(1)}, f32[1,144,2,144]{3,1,2,0:T(8,128)}, u32[]{:S(2)}) copy-start(f32[1,144,2,144]{3,1,2,0:T(8,128)} %get-tuple-element.22) | copy-start | bytes 497668
  470.5 48.3 %copy-start.2 = (f32[1,144,2,144]{3,1,2,0:T(8,128)S(1)}, f32[1,144,2,144]{3,1,2,0:T(8,128)}, u32[]{:S(2)}) copy-start(f32[1,144,2,144]{3,1,2,0:T(8,128)} %get-tuple-element.23) | copy-start | bytes 497668
  655.0 20.4 %all-to-all-start.1 = ((f32[8,1,18432]{2,1,0:T(1,128)}), f32[8,1,18432]{2,1,0:T(1,128)S(1)}, u32[]{:S(2)}, u32[]{:S(2)}) async-start(f32[8,1,18432]{2,1,0:T(1,128)} %reshape.509), calls=%async_computation.1 | async-start | bytes 1179648 | tf_op jit(solution)/shard_map/all_to_all | solution.py:80
  1254.4 10.6 copy-start.5
  1254.4 10.6 copy-start.6
  1254.4 10.6 copy-start.7
Sparse Core Ops, SparseCore 0:
  167.1 29.1 all-gather.1
where the time goes:
time: 1330 us; the launch traced here: 1310 us
  local copies, waits for them, and re-layouts  1010 us (76%)
  matrix products  195 us (15%)
  blocking collectives  40.1 us (3%)
  other arithmetic  36.3 us (3%)
  between operations  14.7 us (1%)
    gather x1, local copies, waits for them, and re-layouts, body(): local_term = freq_space[:, :, stick_heights, stick_slots] / grid_total  532 us
    scatter x1, local copies, waits for them, and re-layouts, body(): flat = jnp.zeros((2, band_count, planes_here, NX * NY), jnp.float32).at[:...  187 us
    unnamed x40, local copies, waits for them, and re-layouts  139 us
    dot_general x1, matrix products, body(): jnp.einsum('pyqv,qbzxv->pbzxy', table_y_out, spatial, precision=HIGHEST)  59.7 us
    another operation x2, local copies, waits for them, and re-layouts  54.4 us
    dot_general x1, matrix products, body(): jnp.einsum('pxqu,qbzuy->pbzxy', table_x_in, spatial, precision=HIGHEST)  48.3 us
    reshape x1, local copies, waits for them, and re-layouts, body(): spatial.reshape(2, band_count, planes_here, NX * NY)[:, :, :, stick_column]  29.2 us
  transfers between devices with their start and end apart: 3, of which 1 were waited for; matrix products, arithmetic and copies ran while one was open for 82% of the time, Pallas kernels for 0%

commit v1 on v0

v1 whole, which is shorter than its diff:
```python
import functools
import math

import jax
import jax.numpy as jnp
import ml_dtypes
import numpy as np
from jax import lax
from jax.experimental import pallas as pl
from jax.experimental.pallas import tpu as pltpu
from jax.sharding import PartitionSpec as P

NX = 144
NY = 144
NZ = 288
HALF = 64
LANES = 128
KINETIC = 8.0
HIGHEST = lax.Precision.HIGHEST
F32 = jnp.float32
BF16 = jnp.bfloat16


def frequency(position, length):
    return jnp.where(position < (length + 1) // 2, position, position - length).astype(F32)


def angles(rows, columns, length):
    phase = np.outer(np.arange(rows), np.arange(columns)) % length
    return 2.0 * np.pi / length * phase


def split_table(table):
    high = table.astype(np.float32).astype(ml_dtypes.bfloat16)
    low = (table - high.astype(np.float64)).astype(np.float32).astype(ml_dtypes.bfloat16)
    return high, low


def plane_table(length):
    angle = angles(length, length, length)
    return split_table(np.concatenate([np.cos(angle), np.sin(angle)], 0))


def normal_tables(devices, planes, padded):
    angle = angles(NZ, NZ, NZ)
    cosine, sine = np.cos(angle), np.sin(angle)
    forward = np.zeros((devices, 2, padded, 2, NZ))
    forward[:, 0, :planes, 0] = cosine.reshape(devices, planes, NZ)
    forward[:, 0, :planes, 1] = -sine.reshape(devices, planes, NZ)
    forward[:, 1, :planes, 0] = sine.reshape(devices, planes, NZ)
    forward[:, 1, :planes, 1] = cosine.reshape(devices, planes, NZ)
    forward = forward.reshape(devices * 2 * padded, 2 * NZ)
    return split_table(forward), split_table(forward.T.copy())


def split_value(value):
    high = value.astype(BF16)
    low = (value - high.astype(F32)).astype(BF16)
    return high, low


def dot3(table_high, table_low, value):
    high, low = split_value(value)
    dot = functools.partial(jnp.dot, preferred_element_type=F32)
    return dot(table_high, high) + dot(table_low, high) + dot(table_high, low)


def projection_kernel(projector_ref, orbital_ref, out_ref):
    pr, pi = projector_ref[0, 0], projector_ref[1, 0]
    orb_r, orb_i = orbital_ref[0, 0], orbital_ref[1, 0]
    out_ref[0, 0:1, :] = jnp.sum(pr * orb_r + pi * orb_i, axis=0, keepdims=True)
    out_ref[0, 1:2, :] = jnp.sum(pr * orb_i - pi * orb_r, axis=0, keepdims=True)


def normal_kernel(planes, orbital_ref, height_ref, high_ref, low_ref, out_ref, dense, slot_heights, slot_values):
    slots, sticks = height_ref.shape
    block = NZ // 2
    base = lax.broadcasted_iota(jnp.int32, (block, LANES), 0)
    for lane in range(0, sticks, LANES):
        slot_heights[...] = height_ref[:, lane : lane + LANES]
        slot_values[0] = orbital_ref[0, 0, :, lane : lane + LANES]
        slot_values[1] = orbital_ref[1, 0, :, lane : lane + LANES]
        for start in range(0, NZ, block):

            def step(slot, carry):
                real, imag = carry
                here = base + start == slot_heights[pl.ds(slot, 1), :]
                row_r = slot_values[0, pl.ds(slot, 1), :]
                row_i = slot_values[1, pl.ds(slot, 1), :]
                return jnp.where(here, row_r, real), jnp.where(here, row_i, imag)

            zero = jnp.zeros((block, LANES), F32)
            real, imag = lax.fori_loop(0, slots, step, (zero, zero), unroll=4)
            dense[start : start + block, lane : lane + LANES] = real
            dense[NZ + start : NZ + start + block, lane : lane + LANES] = imag
    result = dot3(high_ref[...], low_ref[...], dense[...])
    devices = out_ref.shape[0]
    padded = result.shape[0] // (2 * devices)
    for device in range(devices):
        for part in range(2):
            first = (device * 2 + part) * padded
            out_ref[device, part] = result[first : first + planes]


def plane_kernel(
    column_ref, received_ref, potential_ref, high_ref, low_ref, out_ref, grid, factor, wide, tall, rows
):
    devices, _, planes, sticks = received_ref.shape
    total = devices * sticks
    points = NX * NY
    lane = lax.broadcasted_iota(jnp.int32, (1, LANES), 1)
    sign = jnp.where(lane < HALF, -1.0, 1.0).astype(F32)

    tall[...] = jnp.zeros_like(tall)
    tall[0:planes, :] = potential_ref[...]

    def lay(index, carry):
        at = pl.ds(pl.multiple_of(index * LANES, LANES), LANES)
        piece = tall[:, at]
        factor[at, :] = jnp.concatenate([piece, piece], 0).T
        return carry

    lax.fori_loop(0, points // LANES, lay, 0, unroll=2)

    wide[...] = jnp.zeros_like(wide)
    for device in range(devices):
        for part in range(2):
            wide[part * HALF : part * HALF + planes, device * sticks : (device + 1) * sticks] = (
                received_ref[device, part]
            )
    for first in range(0, total, LANES):
        rows[first : first + LANES, :] = wide[:, first : first + LANES].T

    def clear(index, carry):
        grid[pl.ds(pl.multiple_of(index * NY, 8), NY), :] = jnp.zeros((NY, LANES), F32)
        return carry

    lax.fori_loop(0, NX, clear, 0)

    def put(stick, carry):
        grid[pl.ds(column_ref[stick], 1), :] = rows[pl.ds(stick, 1), :]
        return carry

    lax.fori_loop(0, total, put, 0, unroll=8)

    def transform(value, direction):
        product = dot3(high_ref[...], low_ref[...], value)
        length = product.shape[0] // 2
        turned = [
            product[:length, i : i + LANES]
            + (direction * sign) * pltpu.roll(product[length:, i : i + LANES], HALF, 1)
            for i in range(0, 2 * LANES, LANES)
        ]
        return turned

    def along_y(direction):
        def step(pair, carry):
            first = pl.ds(pl.multiple_of(pair * 2 * NY, 8), NY)
            second = pl.ds(pl.multiple_of((pair * 2 + 1) * NY, 8), NY)
            left, right = transform(jnp.concatenate([grid[first, :], grid[second, :]], 1), direction)
            grid[first, :] = left
            grid[second, :] = right
            return carry

        lax.fori_loop(0, NX // 2, step, 0)

    def along_x(pair, carry):
        first = pl.ds(pair * 2, NX, stride=NY)
        second = pl.ds(pair * 2 + 1, NX, stride=NY)
        left, right = transform(jnp.concatenate([grid[first, :], grid[second, :]], 1), 1.0)
        left = left * factor[first, :]
        right = right * factor[second, :]
        left, right = transform(jnp.concatenate([left, right], 1), -1.0)
        grid[first, :] = left
        grid[second, :] = right
        return carry

    along_y(1.0)
    lax.fori_loop(0, NY // 2, along_x, 0)
    along_y(-1.0)

    def take(stick, carry):
        rows[pl.ds(stick, 1), :] = grid[pl.ds(column_ref[stick], 1), :]
        return carry

    lax.fori_loop(0, total, take, 0, unroll=8)
    for first in range(0, total, LANES):
        device, start = first // sticks, first % sticks
        piece = rows[first : first + LANES, :].T
        for part in range(2):
            out_ref[device, part, :, start : start + LANES] = piece[
                part * HALF : part * HALF + planes
            ]


def final_kernel(
    weight_ref,
    back_ref,
    high_ref,
    low_ref,
    height_ref,
    plane_kinetic_ref,
    orbital_ref,
    projector_ref,
    all_ref,
    out_ref,
    sum_ref,
    packed,
    spectrum,
):
    devices, _, planes, sticks = back_ref.shape
    padded = packed.shape[0] // (2 * devices)
    slots = height_ref.shape[0]
    projector_count = projector_ref.shape[1]
    band_total = all_ref.shape[1]
    grid_total = NX * NY * NZ
    packed[...] = jnp.zeros_like(packed)
    for device in range(devices):
        for part in range(2):
            first = (device * 2 + part) * padded
            packed[first : first + planes, :] = back_ref[device, part]
    result = dot3(high_ref[...], low_ref[...], packed[...])
    for lane in range(0, sticks, LANES):
        spectrum[lane // LANES] = result[:, lane : lane + LANES]
    for lane in range(0, sticks, LANES):
        lanes = slice(lane, lane + LANES)
        heights = height_ref[:, lanes]

        def step(height, carry):
            real, imag = carry
            here = heights == height
            row_r = spectrum[lane // LANES, pl.ds(height, 1), :]
            row_i = spectrum[lane // LANES, pl.ds(NZ + height, 1), :]
            return jnp.where(here, row_r, real), jnp.where(here, row_i, imag)

        zero = jnp.zeros((slots, LANES), F32)
        real, imag = lax.fori_loop(0, NZ, step, (zero, zero), unroll=4)
        out_ref[0, 0, :, lanes] = real / grid_total
        out_ref[1, 0, :, lanes] = imag / grid_total
    row_count = 48
    for first in range(0, slots, row_count):
        at = slice(first, first + row_count)
        for lane in range(0, sticks, LANES):
            lanes = slice(lane, lane + LANES)
            along_z = frequency(height_ref[at, lanes], NZ) / NZ
            kinetic = plane_kinetic_ref[:, lanes] + KINETIC * along_z * along_z
            real = jnp.zeros((row_count, LANES), F32)
            imag = jnp.zeros((row_count, LANES), F32)
            for k in range(projector_count):
                pr = projector_ref[0, k, at, lanes]
                pi = projector_ref[1, k, at, lanes]
                wr, wi = weight_ref[0, k], weight_ref[1, k]
                real = real + (pr * wr - pi * wi)
                imag = imag + (pr * wi + pi * wr)
            out_ref[0, 0, at, lanes] = (
                kinetic * orbital_ref[0, 0, at, lanes] + out_ref[0, 0, at, lanes] + real
            )
            out_ref[1, 0, at, lanes] = (
                kinetic * orbital_ref[1, 0, at, lanes] + out_ref[1, 0, at, lanes] + imag
            )
    for band in range(band_total):
        hr, hi = out_ref[0, 0], out_ref[1, 0]
        br, bi = all_ref[0, band], all_ref[1, band]
        sum_ref[0, band : band + 1, :] = jnp.sum(br * hr + bi * hi, axis=0, keepdims=True)
        sum_ref[1, band : band + 1, :] = jnp.sum(br * hi - bi * hr, axis=0, keepdims=True)


def params(mebibytes):
    return pltpu.CompilerParams(vmem_limit_bytes=mebibytes << 20)


def body(orbitals, potential, projectors, coupling, stick_column, stick_heights, projector_atom):
    slot_count = orbitals.shape[2]
    sticks_here = orbitals.shape[3]
    projector_count = projectors.shape[1]
    planes_here = potential.shape[0]
    devices = NZ // planes_here
    stick_total = stick_column.shape[0]
    coeff_total = slot_count * stick_total
    padded = -(-planes_here // 8) * 8
    packed_rows = devices * 2 * padded
    vmem = pl.BlockSpec(memory_space=pltpu.VMEM)
    smem = pl.BlockSpec(memory_space=pltpu.SMEM)
    (z_high, z_low), (back_high, back_low) = normal_tables(devices, planes_here, padded)
    plane_high, plane_low = plane_table(NX)

    all_orbitals = lax.all_gather(orbitals, "band", axis=1, tiled=True)
    band_total = all_orbitals.shape[1]
    first_stick = lax.axis_index("fft") * sticks_here
    local_columns = lax.dynamic_slice_in_dim(stick_column, first_stick, sticks_here)
    along_x = frequency(local_columns // NY, NX) / NX
    along_y = frequency(local_columns % NY, NY) / NY
    plane_kinetic = (KINETIC * (along_x * along_x + along_y * along_y))[None, :]

    block = (2, 1, slot_count, sticks_here)
    partial = pl.pallas_call(
        projection_kernel,
        grid=(projector_count,),
        in_specs=[
            pl.BlockSpec(block, lambda k: (0, k, 0, 0)),
            pl.BlockSpec(block, lambda k: (0, 0, 0, 0)),
        ],
        out_specs=pl.BlockSpec((1, 2, sticks_here), lambda k: (k, 0, 0)),
        out_shape=jax.ShapeDtypeStruct((projector_count, 2, sticks_here), F32),
        compiler_params=params(16),
        cost_estimate=pl.CostEstimate(flops=5000000, bytes_accessed=5000000, transcendentals=0),
    )(projectors, orbitals)
    norm_scale = 1.0 / math.sqrt(coeff_total)
    partial = jnp.sum(partial, axis=2).T[:, :, None]
    projections = lax.psum(partial, "fft") * norm_scale
    same_atom = projector_atom[:, None] == projector_atom[None, :]
    atom_coupling = jnp.where(same_atom, 0.5 * (coupling + coupling.T), jnp.zeros_like(coupling))
    weighted = jnp.einsum("kl,plb->pkb", atom_coupling, projections, precision=HIGHEST)

    exchange = (devices, 2, planes_here, sticks_here)
    z_space = pl.pallas_call(
        functools.partial(normal_kernel, planes_here),
        in_specs=[vmem] * 4,
        out_specs=vmem,
        out_shape=jax.ShapeDtypeStruct(exchange, F32),
        scratch_shapes=[
            pltpu.VMEM((2 * NZ, sticks_here), F32),
            pltpu.VMEM((slot_count, LANES), jnp.int32),
            pltpu.VMEM((2, slot_count, LANES), F32),
        ],
        compiler_params=params(24),
        cost_estimate=pl.CostEstimate(flops=600000000, bytes_accessed=3000000, transcendentals=0),
    )(orbitals, stick_heights, z_high, z_low)
    received = lax.all_to_all(z_space, "fft", split_axis=0, concat_axis=0, tiled=True)
    values = pl.pallas_call(
        plane_kernel,
        in_specs=[smem] + [vmem] * 4,
        out_specs=vmem,
        out_shape=jax.ShapeDtypeStruct(exchange, F32),
        scratch_shapes=[
            pltpu.VMEM((NX * NY, LANES), F32),
            pltpu.VMEM((NX * NY, LANES), F32),
            pltpu.VMEM((2 * HALF, stick_total), F32),
            pltpu.VMEM((HALF, NX * NY), F32),
            pltpu.VMEM((stick_total, LANES), F32),
        ],
        compiler_params=params(56),
        cost_estimate=pl.CostEstimate(
            flops=60000000000, bytes_accessed=6000000, transcendentals=0
        ),
    )(stick_column, received, potential, plane_high, plane_low)
    results = lax.all_to_all(values, "fft", split_axis=0, concat_axis=0, tiled=True)
    applied_h, sums = pl.pallas_call(
        final_kernel,
        in_specs=[smem] + [vmem] * 8,
        out_specs=(vmem, vmem),
        out_shape=(
            jax.ShapeDtypeStruct(orbitals.shape, F32),
            jax.ShapeDtypeStruct((2, band_total, sticks_here), F32),
        ),
        scratch_shapes=[
            pltpu.VMEM((packed_rows, sticks_here), F32),
            pltpu.VMEM((sticks_here // LANES, 2 * NZ, LANES), F32),
        ],
        compiler_params=params(40),
        cost_estimate=pl.CostEstimate(flops=600000000, bytes_accessed=9000000, transcendentals=0),
    )(
        weighted[:, :, 0] * norm_scale,
        results,
        back_high,
        back_low,
        stick_heights,
        plane_kinetic,
        orbitals,
        projectors,
        all_orbitals,
    )
    column = jnp.sum(sums, axis=2)[:, :, None]
    mine = jnp.arange(band_total) == lax.axis_index("band")
    spread = jnp.where(mine[None, None, :], column, jnp.zeros_like(column))
    subspace = lax.psum(spread, ("band", "fft")) / coeff_total
    return (applied_h, projections, subspace)


def solution(mesh):
    in_specs = (
        P(None, "band", None, "fft"),
        P("fft", None),
        P(None, None, None, "fft"),
        P(),
        P(),
        P(None, "fft"),
        P(),
    )
    out_specs = (P(None, "band", None, "fft"), P(None, None, "band"), P())
    return jax.shard_map(body, mesh=mesh, in_specs=in_specs, out_specs=out_specs, check_vma=False)
```

time: 1330 us -> 266 us (0.20); the launches traced: 1310 us -> 265 us
  local copies, waits for them, and re-layouts: 1010 us -> 14.7 us
  matrix products: 195 us -> 0.2 us
  Pallas kernels: 0 us -> 149 us
  other arithmetic: 36.3 us -> 2.2 us
  blocking collectives: 40.1 us -> 57.6 us
    gather x2 -> x0, local copies, waits for them, and re-layouts: 554 us -> none  [the longest x1 532 us: body(): local_term = freq_space[:, :, stick_heights, stick_slots] / grid_total]
    dot_general x9 -> x0, matrix products: 195 us -> none  [the longest x1 59.7 us: body(): jnp.einsum('pyqv,qbzxv->pbzxy', table_y_out, spatial, precision=HIGHEST)]
    scatter x1 -> x0, local copies, waits for them, and re-layouts: 187 us -> none  [body(): flat = jnp.zeros((2, band_count, planes_here, NX * NY), jnp.float32).at[:...]
    pallas_call x0 -> x4, Pallas kernels: none -> 149 us  [the longest x1 131 us: body(): pl.pallas_call(plane_kernel, in_specs=[smem] + [vmem] * 4, out_specs=vmem...]
    unnamed x40 -> x27, local copies, waits for them, and re-layouts: 139 us -> 10.2 us
    another operation x2 -> x0, local copies, waits for them, and re-layouts: 54.4 us -> none
    reshape x1 -> x0, local copies, waits for them, and re-layouts: 29.2 us -> none  [body(): spatial.reshape(2, band_count, planes_here, NX * NY)[:, :, :, stick_column]]
    psum x2, blocking collectives: 32.1 us -> 57.6 us  [the longest x1 39.9 us: body(): subspace = lax.psum(spread, ('band', 'fft')) / coeff_total]
  transfers between devices with their start and end apart: 3 -> 3, of which waited for: 1 -> 1; matrix products, arithmetic and copies ran while one was open for 82% -> 2% of each run, Pallas kernels for 0% -> 50%
where the time goes in v1:
time: 266 us; the launch traced here: 265 us
  Pallas kernels  149 us (56%)
  blocking collectives  57.6 us (22%)
  waiting for transfers between devices  16.7 us (6%)
  local copies, waits for them, and re-layouts  14.7 us (6%)
  between operations  14.2 us (5%)
  starting transfers between devices  10 us (4%)
    pallas_call x1, Pallas kernels, body(): pl.pallas_call(plane_kernel, in_specs=[smem] + [vmem] * 4, out_specs=vmem...  131 us
    psum x1, blocking collectives, body(): subspace = lax.psum(spread, ('band', 'fft')) / coeff_total  39.9 us
    psum x1, blocking collectives, body(): projections = lax.psum(partial, 'fft') * norm_scale  17.7 us
    all_to_all x1, waiting for transfers between devices, body(): lax.all_to_all(z_space, 'fft', split_axis=0, concat_axis=0, tiled=True)  16 us
    unnamed x27, local copies, waits for them, and re-layouts  10.2 us
    pallas_call x1, Pallas kernels, body(): pl.pallas_call(final_kernel, in_specs=[smem] + [vmem] * 8, out_specs=(vme...  8.87 us
    pallas_call x1, Pallas kernels, body(): pl.pallas_call(functools.partial(normal_kernel, planes_here), in_specs=[v...  7.72 us
    all_to_all x1, starting transfers between devices, body(): lax.all_to_all(z_space, 'fft', split_axis=0, concat_axis=0, tiled=True)  6.33 us
  transfers between devices with their start and end apart: 3, of which 1 were waited for; matrix products, arithmetic and copies ran while one was open for 2% of the time, Pallas kernels for 50%

profile of v1, /device:TPU:0, one launch (start us, length us, event | category | flops | bytes accessed | tf_op | source)
XLA Modules:
  0.0 264.9 jit_solution(14719287581103134963)
XLA Ops:
  7.2 1.0 copy-done.2
  8.1 1.1 copy-done.5
  9.3 1.1 copy-done.6
  10.4 0.9 copy-done.9
  11.3 7.7 %shard_map.149 = f32[8,2,36,256]{3,2,1,0:T(8,128)S(1)} custom-call(f32[2,1,144,256]{3,2,1,0:T(8,128)S(1)} %copy-done.2, s32[144,256]{1,0:T(8,128)S(1)} %copy-done.9, bf16[640,576]{1,0:T(8,128)(2,1)S(1)} %copy-done.5, bf16[640,576]{1,0:T(8,128)(2,1)S(1)} %copy-done.6), custom_call_target="tpu_custom_call" | custom-call | flops 600000000 | bytes 3000000 | tf_op jit(solution)/shard_map/pallas_call | solution.py:316
  19.1 1.1 copy.20
  20.2 6.3 %all-to-all-start = ((f32[8,2,36,256]{3,1,2,0:T(2,128)}), f32[8,2,36,256]{3,1,2,0:T(2,128)S(1)}, u32[]{:S(2)}, u32[]{:S(2)}) async-start(f32[8,2,36,256]{3,1,2,0:T(2,128)} %copy.20), calls=%async_computation | async-start | bytes 1179648 | tf_op jit(solution)/shard_map/all_to_all | solution.py:329
  26.5 0.0 all-gather.2.cloned.1.call-start
  26.6 0.7 all-gather.2.cloned.1.call-update
  27.3 16.0 %all-to-all-done = f32[8,2,36,256]{3,1,2,0:T(2,128)S(1)} async-done(((f32[8,2,36,256]{3,1,2,0:T(2,128)}), f32[8,2,36,256]{3,1,2,0:T(2,128)S(1)}, u32[]{:S(2)}, u32[]{:S(2)}) %all-to-all-start) | async-done | bytes 589856 | tf_op jit(solution)/shard_map/all_to_all | solution.py:329
  43.3 0.9 copy.21.received_ref
  44.2 131.1 %shard_map.150 = f32[8,2,36,256]{3,2,1,0:T(8,128)} custom-call(s32[2048]{0:T(1024)} %column_ref.1, f32[8,2,36,256]{3,2,1,0:T(8,128)} %copy.21.received_ref, f32[36,20736]{1,0:T(8,128)} %potential_ref.1, bf16[288,144]{1,0:T(8,128)(2,1)} %constant.71.clone.high_ref, bf16[288,144]{1,0:T(8,128)(2,1)} %constant.72.clone.low_ref), custom_call_target="tpu_custom_call" | custom-call | flops 60000002048 | bytes 6000000 | tf_op jit(solution)/shard_map/pallas_call | solution.py:330
  175.3 2.3 copy.22
  177.6 3.7 %all-to-all-start.1 = ((f32[8,2,36,256]{3,1,2,0:T(2,128)}), f32[8,2,36,256]{3,1,2,0:T(2,128)S(1)}, u32[]{:S(2)}, u32[]{:S(2)}) async-start(f32[8,2,36,256]{3,1,2,0:T(2,128)} %copy.22), calls=%async_computation.1 | async-start | bytes 1179648 | tf_op jit(solution)/shard_map/all_to_all | solution.py:347
  181.3 2.3 copy-done
  183.7 1.6 shard_map.148
  185.3 0.1 reduce_sum.18
  185.4 0.1 copy.18
  185.5 0.1 copy.19
  185.6 17.7 %psum.14 = f32[2,16,1]{1,0,2:T(2,128)S(1)} all-reduce(f32[2,16,1]{1,0,2:T(2,128)S(1)} %bitcast.16), channel_id=1, replica_groups=mesh['band'=4,'fft'=8] {'fft'}, use_global_device_ids=true, to_apply=%region_1.2 | all-reduce | flops 32 | bytes 256 | tf_op jit(solution)/shard_map/psum | solution.py:310
  203.2 0.8 fusion.13
  204.0 0.2 convolution_multiply_fusion.weight_ref
  204.2 0.1 copy.23.back_ref
  204.3 0.0 all-gather.2.cloned.1.call-done.all_ref
  204.4 2.3 copy-done.1
  206.7 1.3 copy-done.4
  208.0 8.9 %shard_map.151 = (f32[2,1,144,256]{3,2,1,0:T(8,128)}, f32[2,4,256]{2,1,0:T(4,128)S(1)}) custom-call(f32[2,16]{1,0:T(2,128)S(1)} %convolution_multiply_fusion.weight_ref, f32[8,2,36,256]{3,2,1,0:T(8,128)S(1)} %copy.23.back_ref, bf16[576,640]{1,0:T(8,128)(2,1)S(1)} %copy-done.7, bf16[576,640]{1,0:T(8,128)(2,1)S(1)} %copy-done.8, s32[144,256]{1,0:T(8,128)S(1)} %copy-done.10, ...), custom_call_target="tpu_custom_call" | custom-call | flops 600000000 | bytes 9000000 | tf_op jit(solution)/shard_map/pallas_call | solution.py:348
  216.8 0.1 reduce_sum.19
  216.9 0.1 broadcast_select_fusion
  217.0 0.6 broadcast_multiply_fusion.1
  217.6 39.9 %psum.15 = f32[2,4,4]{2,1,0:T(4,128)S(1)} all-reduce(f32[2,4,4]{2,1,0:T(4,128)S(1)} %broadcast_select_fusion), channel_id=1, replica_groups=mesh['band'=4,'fft'=8] {'band','fft'}, use_global_device_ids=true, to_apply=%region_3.4 | all-reduce | flops 32 | bytes 256 | tf_op jit(solution)/shard_map/psum | solution.py:376
  257.5 0.6 broadcast_multiply_fusion
  (21 shorter events, 0.0 us)
Async XLA Ops:
  7.2 1.0 copy-start.2
  8.1 1.1 copy-start.5
  9.3 1.1 copy-start.6
  10.4 0.9 copy-start.9
  20.2 23.1 %all-to-all-start = ((f32[8,2,36,256]{3,1,2,0:T(2,128)}), f32[8,2,36,256]{3,1,2,0:T(2,128)S(1)}, u32[]{:S(2)}, u32[]{:S(2)}) async-start(f32[8,2,36,256]{3,1,2,0:T(2,128)} %copy.20), calls=%async_computation | async-start | bytes 1179648 | tf_op jit(solution)/shard_map/all_to_all | solution.py:329
  26.5 177.8 %all-gather.2.cloned.1.call-start = ((), (), s32[]{:S(2)}) async-start(), calls=%async_computation.2 | async-start | bytes 1474560 | tf_op jit(solution)/shard_map/all_gather | solution.py:287
  44.2 137.1 %copy-start.3 = (f32[2,1,144,256]{3,2,1,0:T(8,128)S(1)}, f32[2,1,144,256]{3,2,1,0:T(8,128)}, u32[]{:S(2)}) copy-start(f32[2,1,144,256]{3,2,1,0:T(8,128)} %orbital_ref.5) | copy-start | bytes 884740
  175.3 29.0 %copy-start.8 = (bf16[576,640]{1,0:T(8,128)(2,1)S(1)}, bf16[576,640]{1,0:T(8,128)(2,1)}, u32[]{:S(2)}) copy-start(bf16[576,640]{1,0:T(8,128)(2,1)} %constant.74.clone.low_ref) | copy-start | bytes 2211844
  177.6 7.9 %copy-start.11 = (f32[16,16]{1,0:T(8,128)S(1)}, f32[16,16]{1,0:T(8,128)}, u32[]{:S(2)}) copy-start(f32[16,16]{1,0:T(8,128)} %param.16) | copy-start | bytes 3076
  177.6 26.4 %copy-start.12 = (s32[16]{0:T(128)S(1)}, s32[16]{0:T(128)}, u32[]{:S(2)}) copy-start(s32[16]{0:T(128)} %param.19) | copy-start | bytes 196
  177.6 26.7 %copy-start.7 = (bf16[576,640]{1,0:T(8,128)(2,1)S(1)}, bf16[576,640]{1,0:T(8,128)(2,1)}, u32[]{:S(2)}) copy-start(bf16[576,640]{1,0:T(8,128)(2,1)} %constant.73.clone.high_ref) | copy-start | bytes 2211844
  177.6 26.7 %copy-start.10 = (s32[144,256]{1,0:T(8,128)S(1)}, s32[144,256]{1,0:T(8,128)}, u32[]{:S(2)}) copy-start(s32[144,256]{1,0:T(8,128)} %height_ref.3) | copy-start | bytes 442372
  177.6 26.6 %all-to-all-start.1 = ((f32[8,2,36,256]{3,1,2,0:T(2,128)}), f32[8,2,36,256]{3,1,2,0:T(2,128)S(1)}, u32[]{:S(2)}, u32[]{:S(2)}) async-start(f32[8,2,36,256]{3,1,2,0:T(2,128)} %copy.22), calls=%async_computation.1 | async-start | bytes 1179648 | tf_op jit(solution)/shard_map/all_to_all | solution.py:347
  181.3 2.3 copy-start
  204.3 2.3 copy-start.1
  206.7 1.3 copy-start.4
Sparse Core Ops, SparseCore 0:
  29.2 29.1 all-gather.1

commit v2 on v1

--- a/solution.py
+++ b/solution.py
@@ -19,6 +19,7 @@
 HIGHEST = lax.Precision.HIGHEST
 F32 = jnp.float32
 BF16 = jnp.bfloat16
+MESH = pl.DeviceIdType.MESH
 
 
 def frequency(position, length):
@@ -65,15 +66,29 @@
     return dot(table_high, high) + dot(table_low, high) + dot(table_high, low)
 
 
-def projection_kernel(projector_ref, orbital_ref, out_ref):
-    pr, pi = projector_ref[0, 0], projector_ref[1, 0]
-    orb_r, orb_i = orbital_ref[0, 0], orbital_ref[1, 0]
-    out_ref[0, 0:1, :] = jnp.sum(pr * orb_r + pi * orb_i, axis=0, keepdims=True)
-    out_ref[0, 1:2, :] = jnp.sum(pr * orb_i - pi * orb_r, axis=0, keepdims=True)
-
-
-def normal_kernel(planes, orbital_ref, height_ref, high_ref, low_ref, out_ref, dense, slot_heights, slot_values):
+def fold(row):
+    return sum(row[:, i : i + LANES] for i in range(0, row.shape[1], LANES))
+
+
+def normal_kernel(
+    planes,
+    orbital_ref,
+    height_ref,
+    high_ref,
+    low_ref,
+    projector_ref,
+    out_ref,
+    dense,
+    slot_heights,
+    slot_values,
+    held,
+    partial,
+    arrived,
+):
     slots, sticks = height_ref.shape
+    projector_count = projector_ref.shape[1]
+    fetch = pltpu.make_async_copy(projector_ref, held, arrived)
+    fetch.start()
     block = NZ // 2
     base = lax.broadcasted_iota(jnp.int32, (block, LANES), 0)
     for lane in range(0, sticks, LANES):
@@ -99,13 +114,31 @@
     for device in range(devices):
         for part in range(2):
             first = (device * 2 + part) * padded
-            out_ref[device, part] = result[first : first + planes]
+            out_ref[device, part * padded : (part + 1) * padded, :] = result[
+                first : first + padded
+            ]
+    fetch.wait()
+    partial[...] = jnp.zeros_like(partial)
+    orb_r, orb_i = orbital_ref[0, 0], orbital_ref[1, 0]
+    for k in range(projector_count):
+        pr, pi = held[0, k], held[1, k]
+        real = jnp.sum(pr * orb_r + pi * orb_i, axis=0, keepdims=True)
+        imag = jnp.sum(pr * orb_i - pi * orb_r, axis=0, keepdims=True)
+        partial[k : k + 1, :] = fold(real)
+        partial[HALF + k : HALF + k + 1, :] = fold(imag)
+    sums = jnp.sum(partial[...].T, axis=0, keepdims=True)
+    sums = jnp.concatenate([sums] + [jnp.zeros_like(sums)] * (sticks // LANES - 1), 1)
+    sums = jnp.broadcast_to(sums, (8, sticks))
+    for device in range(devices):
+        out_ref[device, 2 * padded :, :] = sums
 
 
 def plane_kernel(
-    column_ref, received_ref, potential_ref, high_ref, low_ref, out_ref, grid, factor, wide, tall, rows
+    column_ref, received_ref, potential_ref, table_ref, out_ref, total_ref, grid, factor, wide, tall, rows
 ):
-    devices, _, planes, sticks = received_ref.shape
+    devices, _, sticks = received_ref.shape
+    planes = potential_ref.shape[0]
+    padded = (received_ref.shape[1] - 8) // 2
     total = devices * sticks
     points = NX * NY
     lane = lax.broadcasted_iota(jnp.int32, (1, LANES), 1)
@@ -120,14 +153,15 @@
         factor[at, :] = jnp.concatenate([piece, piece], 0).T
         return carry
 
-    lax.fori_loop(0, points // LANES, lay, 0, unroll=2)
+    lax.fori_loop(0, points // LANES, lay, 0, unroll=9)
 
     wide[...] = jnp.zeros_like(wide)
     for device in range(devices):
         for part in range(2):
-            wide[part * HALF : part * HALF + planes, device * sticks : (device + 1) * sticks] = (
-                received_ref[device, part]
+            wide[part * HALF : part * HALF + padded, device * sticks : (device + 1) * sticks] = (
+                received_ref[device, part * padded : (part + 1) * padded, :]
             )
+    total_ref[...] = sum(received_ref[device, 2 * padded :, 0:LANES] for device in range(devices))
     for first in range(0, total, LANES):
         rows[first : first + LANES, :] = wide[:, first : first + LANES].T
 
@@ -135,16 +169,19 @@
         grid[pl.ds(pl.multiple_of(index * NY, 8), NY), :] = jnp.zeros((NY, LANES), F32)
         return carry
 
-    lax.fori_loop(0, NX, clear, 0)
+    lax.fori_loop(0, NX, clear, 0, unroll=4)
 
     def put(stick, carry):
         grid[pl.ds(column_ref[stick], 1), :] = rows[pl.ds(stick, 1), :]
         return carry
 
-    lax.fori_loop(0, total, put, 0, unroll=8)
+    lax.fori_loop(0, total, put, 0, unroll=16)
 
     def transform(value, direction):
-        product = dot3(high_ref[...], low_ref[...], value)
+        high, low = split_value(value)
+        product = jnp.dot(
+            table_ref[...], jnp.concatenate([high, low, high], 0), preferred_element_type=F32
+        )
         length = product.shape[0] // 2
         turned = [
             product[:length, i : i + LANES]
@@ -162,7 +199,7 @@
             grid[second, :] = right
             return carry
 
-        lax.fori_loop(0, NX // 2, step, 0)
+        lax.fori_loop(0, NX // 2, step, 0, unroll=6)
 
     def along_x(pair, carry):
         first = pl.ds(pair * 2, NX, stride=NY)
@@ -176,7 +213,7 @@
         return carry
 
     along_y(1.0)
-    lax.fori_loop(0, NY // 2, along_x, 0)
+    lax.fori_loop(0, NY // 2, along_x, 0, unroll=6)
     along_y(-1.0)
 
     def take(stick, carry):
@@ -188,8 +225,8 @@
         device, start = first // sticks, first % sticks
         piece = rows[first : first + LANES, :].T
         for part in range(2):
-            out_ref[device, part, :, start : start + LANES] = piece[
-                part * HALF : part * HALF + planes
+            out_ref[device, part * padded : (part + 1) * padded, start : start + LANES] = piece[
+                part * HALF : part * HALF + padded
             ]
 
 
@@ -205,21 +242,16 @@
     all_ref,
     out_ref,
     sum_ref,
-    packed,
     spectrum,
 ):
-    devices, _, planes, sticks = back_ref.shape
-    padded = packed.shape[0] // (2 * devices)
+    devices, double, sticks = back_ref.shape
+    padded = double // 2
     slots = height_ref.shape[0]
     projector_count = projector_ref.shape[1]
     band_total = all_ref.shape[1]
     grid_total = NX * NY * NZ
-    packed[...] = jnp.zeros_like(packed)
-    for device in range(devices):
-        for part in range(2):
-            first = (device * 2 + part) * padded
-            packed[first : first + planes, :] = back_ref[device, part]
-    result = dot3(high_ref[...], low_ref[...], packed[...])
+    back = back_ref[...].reshape(devices * 2 * padded, sticks)
+    result = dot3(high_ref[...], low_ref[...], back)
     for lane in range(0, sticks, LANES):
         spectrum[lane // LANES] = result[:, lane : lane + LANES]
     for lane in range(0, sticks, LANES):
@@ -265,6 +297,57 @@
         sum_ref[1, band : band + 1, :] = jnp.sum(br * hi - bi * hr, axis=0, keepdims=True)
 
 
+def gather_kernel(
+    fft_count, band_count, sum_ref, out_ref, own, summed, fft_in, band_in, fs, fr, bs, br
+):
+    fft, band = lax.axis_index("fft"), lax.axis_index("band")
+    barrier = pltpu.get_barrier_semaphore()
+    for i in range(1, fft_count):
+        pl.semaphore_signal(
+            barrier, inc=1, device_id=(band, lax.rem(fft + i, fft_count)), device_id_type=MESH
+        )
+    for i in range(1, band_count):
+        pl.semaphore_signal(
+            barrier, inc=1, device_id=(lax.rem(band + i, band_count), fft), device_id_type=MESH
+        )
+    own[...] = fold(sum_ref[...])
+    pl.semaphore_wait(barrier, fft_count + band_count - 2)
+
+    def exchange(count, source, slots, send, receive, target):
+        copies = []
+        for i in range(1, count):
+            copy = pltpu.make_async_remote_copy(
+                src_ref=source,
+                dst_ref=slots.at[i],
+                send_sem=send.at[i],
+                recv_sem=receive.at[i],
+                device_id=target(i),
+                device_id_type=MESH,
+            )
+            copy.start()
+            copies.append(copy)
+        return copies
+
+    copies = exchange(
+        fft_count, own, fft_in, fs, fr, lambda i: (band, lax.rem(fft + i, fft_count))
+    )
+    for copy in copies:
+        copy.wait()
+    fft_in[0] = own[...]
+    total = jnp.zeros_like(own)
+    for i in range(fft_count):
+        total = total + fft_in[lax.rem(fft - i + fft_count, fft_count)]
+    summed[...] = total
+    copies = exchange(
+        band_count, summed, band_in, bs, br, lambda i: (lax.rem(band + i, band_count), fft)
+    )
+    for copy in copies:
+        copy.wait()
+    band_in[0] = summed[...]
+    for i in range(band_count):
+        out_ref[i] = band_in[lax.rem(band - i + band_count, band_count)]
+
+
 def params(mebibytes):
     return pltpu.CompilerParams(vmem_limit_bytes=mebibytes << 20)
 
@@ -278,11 +361,11 @@
     stick_total = stick_column.shape[0]
     coeff_total = slot_count * stick_total
     padded = -(-planes_here // 8) * 8
-    packed_rows = devices * 2 * padded
     vmem = pl.BlockSpec(memory_space=pltpu.VMEM)
     smem = pl.BlockSpec(memory_space=pltpu.SMEM)
     (z_high, z_low), (back_high, back_low) = normal_tables(devices, planes_here, padded)
     plane_high, plane_low = plane_table(NX)
+    plane_triple = np.concatenate([plane_high, plane_high, plane_low], 1)
 
     all_orbitals = lax.all_gather(orbitals, "band", axis=1, tiled=True)
     band_total = all_orbitals.shape[1]
@@ -292,46 +375,31 @@
     along_y = frequency(local_columns % NY, NY) / NY
     plane_kinetic = (KINETIC * (along_x * along_x + along_y * along_y))[None, :]
 
-    block = (2, 1, slot_count, sticks_here)
-    partial = pl.pallas_call(
-        projection_kernel,
-        grid=(projector_count,),
-        in_specs=[
-            pl.BlockSpec(block, lambda k: (0, k, 0, 0)),
-            pl.BlockSpec(block, lambda k: (0, 0, 0, 0)),
-        ],
-        out_specs=pl.BlockSpec((1, 2, sticks_here), lambda k: (k, 0, 0)),
-        out_shape=jax.ShapeDtypeStruct((projector_count, 2, sticks_here), F32),
-        compiler_params=params(16),
-        cost_estimate=pl.CostEstimate(flops=5000000, bytes_accessed=5000000, transcendentals=0),
-    )(projectors, orbitals)
-    norm_scale = 1.0 / math.sqrt(coeff_total)
-    partial = jnp.sum(partial, axis=2).T[:, :, None]
-    projections = lax.psum(partial, "fft") * norm_scale
-    same_atom = projector_atom[:, None] == projector_atom[None, :]
-    atom_coupling = jnp.where(same_atom, 0.5 * (coupling + coupling.T), jnp.zeros_like(coupling))
-    weighted = jnp.einsum("kl,plb->pkb", atom_coupling, projections, precision=HIGHEST)
-
-    exchange = (devices, 2, planes_here, sticks_here)
+    forth = (devices, 2 * padded + 8, sticks_here)
+    back = (devices, 2 * padded, sticks_here)
+    anywhere = pl.BlockSpec(memory_space=pl.ANY)
     z_space = pl.pallas_call(
         functools.partial(normal_kernel, planes_here),
-        in_specs=[vmem] * 4,
+        in_specs=[vmem] * 4 + [anywhere],
         out_specs=vmem,
-        out_shape=jax.ShapeDtypeStruct(exchange, F32),
+        out_shape=jax.ShapeDtypeStruct(forth, F32),
         scratch_shapes=[
             pltpu.VMEM((2 * NZ, sticks_here), F32),
             pltpu.VMEM((slot_count, LANES), jnp.int32),
             pltpu.VMEM((2, slot_count, LANES), F32),
+            pltpu.VMEM(projectors.shape, F32),
+            pltpu.VMEM((LANES, LANES), F32),
+            pltpu.SemaphoreType.DMA,
         ],
         compiler_params=params(24),
         cost_estimate=pl.CostEstimate(flops=600000000, bytes_accessed=3000000, transcendentals=0),
-    )(orbitals, stick_heights, z_high, z_low)
+    )(orbitals, stick_heights, z_high, z_low, projectors)
     received = lax.all_to_all(z_space, "fft", split_axis=0, concat_axis=0, tiled=True)
-    values = pl.pallas_call(
+    values, total = pl.pallas_call(
         plane_kernel,
-        in_specs=[smem] + [vmem] * 4,
-        out_specs=vmem,
-        out_shape=jax.ShapeDtypeStruct(exchange, F32),
+        in_specs=[smem] + [vmem] * 3,
+        out_specs=(vmem, vmem),
+        out_shape=(jax.ShapeDtypeStruct(back, F32), jax.ShapeDtypeStruct((8, LANES), F32)),
         scratch_shapes=[
             pltpu.VMEM((NX * NY, LANES), F32),
             pltpu.VMEM((NX * NY, LANES), F32),
@@ -343,7 +411,13 @@
         cost_estimate=pl.CostEstimate(
             flops=60000000000, bytes_accessed=6000000, transcendentals=0
         ),
-    )(stick_column, received, potential, plane_high, plane_low)
+    )(stick_column, received, potential, plane_triple)
+    norm_scale = 1.0 / math.sqrt(coeff_total)
+    total = total[0].reshape(2, HALF)[:, :projector_count, None]
+    projections = total * norm_scale
+    same_atom = projector_atom[:, None] == projector_atom[None, :]
+    atom_coupling = jnp.where(same_atom, 0.5 * (coupling + coupling.T), jnp.zeros_like(coupling))
+    weighted = jnp.einsum("kl,plb->pkb", atom_coupling, projections, precision=HIGHEST)
     results = lax.all_to_all(values, "fft", split_axis=0, concat_axis=0, tiled=True)
     applied_h, sums = pl.pallas_call(
         final_kernel,
@@ -354,7 +428,6 @@
             jax.ShapeDtypeStruct((2, band_total, sticks_here), F32),
         ),
         scratch_shapes=[
-            pltpu.VMEM((packed_rows, sticks_here), F32),
             pltpu.VMEM((sticks_here // LANES, 2 * NZ, LANES), F32),
         ],
         compiler_params=params(40),
@@ -370,10 +443,27 @@
         projectors,
         all_orbitals,
     )
-    column = jnp.sum(sums, axis=2)[:, :, None]
-    mine = jnp.arange(band_total) == lax.axis_index("band")
-    spread = jnp.where(mine[None, None, :], column, jnp.zeros_like(column))
-    subspace = lax.psum(spread, ("band", "fft")) / coeff_total
+    band_devices = band_total // orbitals.shape[1]
+    rows = 2 * band_total
+    gathered = pl.pallas_call(
+        functools.partial(gather_kernel, devices, band_devices),
+        in_specs=[vmem],
+        out_specs=vmem,
+        out_shape=jax.ShapeDtypeStruct((band_devices, rows, LANES), F32),
+        scratch_shapes=[
+            pltpu.VMEM((rows, LANES), F32),
+            pltpu.VMEM((rows, LANES), F32),
+            pltpu.VMEM((devices, rows, LANES), F32),
+            pltpu.VMEM((band_devices, rows, LANES), F32),
+            pltpu.SemaphoreType.DMA((devices,)),
+            pltpu.SemaphoreType.DMA((devices,)),
+            pltpu.SemaphoreType.DMA((band_devices,)),
+            pltpu.SemaphoreType.DMA((band_devices,)),
+        ],
+        compiler_params=pltpu.CompilerParams(collective_id=0, has_side_effects=True),
+    )(sums.reshape(rows, sticks_here))
+    subspace = jnp.sum(gathered, axis=2).reshape(band_devices, 2, band_total)
+    subspace = jnp.transpose(subspace, (1, 2, 0)) / coeff_total
     return (applied_h, projections, subspace)
 
 

time: 266 us -> 158 us (0.59)
  Pallas kernels: 149 us -> 82.7 us
  blocking collectives: 57.6 us -> 0 us
  waiting for transfers between devices: 16.7 us -> 35.1 us
    pallas_call x2, Pallas kernels: 133 us -> 64.1 us  [the longest x1 53.1 us: body(): pl.pallas_call(plane_kernel, in_specs=[smem] + [vmem] * 3, out_specs=(vme...]
    psum x2 -> x0, blocking collectives: 57.6 us -> none  [the longest x1 39.9 us: body(): subspace = lax.psum(spread, ('band', 'fft')) / coeff_total]
    all_to_all x1, waiting for transfers between devices: 0.01 us -> 15.7 us  [body(): lax.all_to_all(values, 'fft', split_axis=0, concat_axis=0, tiled=True)]
    pallas_call x2 -> x0, local copies, waits for them, and re-layouts: 3.42 us -> none  [the longest x1 2.28 us: body(): pl.pallas_call(plane_kernel, in_specs=[smem] + [vmem] * 4, out_specs=vmem...]
    all_to_all x1, waiting for transfers between devices: 16 us -> 18.8 us  [body(): lax.all_to_all(z_space, 'fft', split_axis=0, concat_axis=0, tiled=True)]
    unnamed x27 -> x30, local copies, waits for them, and re-layouts: 10.2 us -> 11.8 us
  transfers between devices with their start and end apart: 3 -> 3, of which waited for: 1 -> 2; matrix products, arithmetic and copies ran while one was open for 2% -> 2% of each run, Pallas kernels for 50% -> 34%
where the time goes in v2:
time: 158 us; the launch traced here: 157 us
  Pallas kernels  82.7 us (52%)
  waiting for transfers between devices  35.1 us (22%)
  between operations  14.2 us (9%)
  local copies, waits for them, and re-layouts  13.2 us (8%)
  starting transfers between devices  9.91 us (6%)
  other arithmetic  2.16 us (1%)
    pallas_call x1, Pallas kernels, body(): pl.pallas_call(plane_kernel, in_specs=[smem] + [vmem] * 3, out_specs=(vme...  53.1 us
    all_to_all x1, waiting for transfers between devices, body(): lax.all_to_all(z_space, 'fft', split_axis=0, concat_axis=0, tiled=True)  18.8 us
    all_to_all x1, waiting for transfers between devices, body(): lax.all_to_all(values, 'fft', split_axis=0, concat_axis=0, tiled=True)  15.7 us
    unnamed x30, local copies, waits for them, and re-layouts  11.8 us
    pallas_call x1, Pallas kernels, body(): pl.pallas_call(functools.partial(gather_kernel, devices, band_devices), i...  11 us
    pallas_call x1, Pallas kernels, body(): pl.pallas_call(functools.partial(normal_kernel, planes_here), in_specs=[v...  9.77 us
    pallas_call x1, Pallas kernels, body(): pl.pallas_call(final_kernel, in_specs=[smem] + [vmem] * 8, out_specs=(vme...  8.83 us
    all_to_all x1, starting transfers between devices, body(): lax.all_to_all(z_space, 'fft', split_axis=0, concat_axis=0, tiled=True)  6.34 us
  transfers between devices with their start and end apart: 3, of which 2 were waited for; matrix products, arithmetic and copies ran while one was open for 2% of the time, Pallas kernels for 34%

profile of v2, /device:TPU:0, one launch (start us, length us, event | category | flops | bytes accessed | tf_op | source)
XLA Modules:
  0.0 157.5 jit_solution(3588418363060976750)
XLA Ops:
  7.2 0.0 copy-start
  7.2 2.3 %copy-done = f32[2,16,144,256]{3,2,1,0:T(8,128)S(1)} copy-done((f32[2,16,144,256]{3,2,1,0:T(8,128)S(1)}, f32[2,16,144,256]{3,2,1,0:T(8,128)}, u32[]{:S(2)}) %copy-start) | copy-done | bytes 4718616
  9.5 1.0 copy-done.2
  10.5 1.1 copy-done.5
  11.6 1.1 copy-done.6
  12.8 0.9 copy-done.9
  13.7 9.8 %shard_map.139 = f32[8,88,256]{2,1,0:T(8,128)} custom-call(f32[2,1,144,256]{3,2,1,0:T(8,128)S(1)} %copy-done.2, s32[144,256]{1,0:T(8,128)S(1)} %copy-done.9, bf16[640,576]{1,0:T(8,128)(2,1)S(1)} %copy-done.5, bf16[640,576]{1,0:T(8,128)(2,1)S(1)} %copy-done.6, f32[2,16,144,256]{3,2,1,0:T(8,128)S(1)} %copy-done), custom_call_target="tpu_custom_call" | custom-call | flops 600000000 | bytes 3000000 | tf_op jit(solution)/shard_map/pallas_call | solution.py:381
  23.4 6.3 %all-to-all-start = ((f32[8,88,256]{2,1,0:T(8,128)}), f32[8,88,256]{2,1,0:T(8,128)S(1)}, u32[]{:S(2)}, u32[]{:S(2)}) async-start(f32[8,88,256]{2,1,0:T(8,128)} %shard_map.139), calls=%async_computation | async-start | bytes 1441792 | tf_op jit(solution)/shard_map/all_to_all | solution.py:397
  29.8 0.0 all-gather.2.cloned.1.call-start
  29.8 0.7 all-gather.2.cloned.1.call-update
  30.5 0.0 copy-start.12
  30.6 0.0 copy-start.7
  30.6 0.0 copy-start.8
  30.6 18.8 %all-to-all-done.received_ref = f32[8,88,256]{2,1,0:T(8,128)S(1)} async-done(((f32[8,88,256]{2,1,0:T(8,128)}), f32[8,88,256]{2,1,0:T(8,128)S(1)}, u32[]{:S(2)}, u32[]{:S(2)}) %all-to-all-start) | async-done | bytes 720928 | tf_op jit(solution)/shard_map/all_to_all | solution.py:397
  49.4 0.9 copy-done.11
  50.2 53.1 %shard_map.140 = (f32[8,80,256]{2,1,0:T(8,128)}, f32[8,128]{1,0:T(8,128)}) custom-call(s32[2048]{0:T(1024)} %column_ref.1, f32[8,88,256]{2,1,0:T(8,128)} %copy-done.11, f32[36,20736]{1,0:T(8,128)} %potential_ref.1, bf16[288,432]{1,0:T(8,128)(2,1)} %constant.64.clone.table_ref), custom_call_target="tpu_custom_call" | custom-call | flops 60000002048 | bytes 6000000 | tf_op jit(solution)/shard_map/pallas_call | solution.py:398
  103.4 3.5 %all-to-all-start.1 = ((f32[8,80,256]{2,1,0:T(8,128)}), f32[8,80,256]{2,1,0:T(8,128)S(1)}, u32[]{:S(2)}, u32[]{:S(2)}) async-start(f32[8,80,256]{2,1,0:T(8,128)} %get-tuple-element.8), calls=%async_computation.1 | async-start | bytes 1310720 | tf_op jit(solution)/shard_map/all_to_all | solution.py:421
  106.9 0.1 copy.15
  107.0 0.8 fusion.12
  107.8 0.7 slice_reduce_fusion
  108.5 0.1 reshape_squeeze.3
  108.6 0.6 slice_multiply_fusion
  109.2 0.2 convolution_multiply_fusion.weight_ref
  109.4 15.7 %all-to-all-done.1.back_ref = f32[8,80,256]{2,1,0:T(8,128)S(1)} async-done(((f32[8,80,256]{2,1,0:T(8,128)}), f32[8,80,256]{2,1,0:T(8,128)S(1)}, u32[]{:S(2)}, u32[]{:S(2)}) %all-to-all-start.1) | async-done | bytes 655392 | tf_op jit(solution)/shard_map/all_to_all | solution.py:421
  125.1 2.3 %copy-done.1 = f32[2,16,144,256]{3,2,1,0:T(8,128)S(1)} copy-done((f32[2,16,144,256]{3,2,1,0:T(8,128)S(1)}, f32[2,16,144,256]{3,2,1,0:T(8,128)}, u32[]{:S(2)}) %copy-start.1) | copy-done | bytes 4718616
  127.4 1.3 copy-done.4
  128.7 8.8 %shard_map.141 = (f32[2,1,144,256]{3,2,1,0:T(8,128)}, f32[2,4,256]{2,1,0:T(4,128)S(1)}) custom-call(f32[2,16]{1,0:T(2,128)S(1)} %convolution_multiply_fusion.weight_ref, f32[8,80,256]{2,1,0:T(8,128)S(1)} %all-to-all-done.1.back_ref, bf16[576,640]{1,0:T(8,128)(2,1)S(1)} %copy-done.7, bf16[576,640]{1,0:T(8,128)(2,1)S(1)} %copy-done.8, ...), custom_call_target="tpu_custom_call" | custom-call | flops 600000000 | bytes 9000000 | tf_op jit(solution)/shard_map/pallas_call | solution.py:422
  137.5 0.6 reshape.19.sum_ref
  138.1 11.0 %shard_map.142 = f32[4,8,128]{2,1,0:T(8,128)} custom-call(f32[8,256]{1,0:T(8,128)} %reshape.19.sum_ref), custom_call_target="tpu_custom_call" | custom-call | tf_op jit(solution)/shard_map/pallas_call | solution.py:448
  149.1 0.8 reduce_sum.9
  149.9 0.1 div.27
  150.0 0.7 copy.17
  (18 shorter events, 0.0 us)
Async XLA Ops:
  7.2 2.3 %copy-start = (f32[2,16,144,256]{3,2,1,0:T(8,128)S(1)}, f32[2,16,144,256]{3,2,1,0:T(8,128)}, u32[]{:S(2)}) copy-start(f32[2,16,144,256]{3,2,1,0:T(8,128)} %projector_ref.3) | copy-start | bytes 14155780
  9.5 1.0 copy-start.2
  10.5 1.1 copy-start.5
  11.6 1.1 copy-start.6
  12.8 0.9 copy-start.9
  23.4 25.9 %all-to-all-start = ((f32[8,88,256]{2,1,0:T(8,128)}), f32[8,88,256]{2,1,0:T(8,128)S(1)}, u32[]{:S(2)}, u32[]{:S(2)}) async-start(f32[8,88,256]{2,1,0:T(8,128)} %shard_map.139), calls=%async_computation | async-start | bytes 1441792 | tf_op jit(solution)/shard_map/all_to_all | solution.py:397
  29.8 79.6 %all-gather.2.cloned.1.call-start = ((), (), s32[]{:S(2)}) async-start(), calls=%async_computation.2 | async-start | bytes 1474560 | tf_op jit(solution)/shard_map/all_gather | solution.py:370
  30.5 76.4 %copy-start.12 = (f32[16,16]{1,0:T(8,128)S(1)}, f32[16,16]{1,0:T(8,128)}, u32[]{:S(2)}) copy-start(f32[16,16]{1,0:T(8,128)} %param.15) | copy-start | bytes 3076
  30.5 78.6 %copy-start.13 = (s32[16]{0:T(128)S(1)}, s32[16]{0:T(128)}, u32[]{:S(2)}) copy-start(s32[16]{0:T(128)} %param.18) | copy-start | bytes 196
  30.5 94.5 %copy-start.3 = (f32[2,1,144,256]{3,2,1,0:T(8,128)S(1)}, f32[2,1,144,256]{3,2,1,0:T(8,128)}, u32[]{:S(2)}) copy-start(f32[2,1,144,256]{3,2,1,0:T(8,128)} %orbital_ref.3) | copy-start | bytes 884740
  30.6 94.5 %copy-start.7 = (bf16[576,640]{1,0:T(8,128)(2,1)S(1)}, bf16[576,640]{1,0:T(8,128)(2,1)}, u32[]{:S(2)}) copy-start(bf16[576,640]{1,0:T(8,128)(2,1)} %constant.65.clone.high_ref) | copy-start | bytes 2211844
  30.6 94.5 %copy-start.8 = (bf16[576,640]{1,0:T(8,128)(2,1)S(1)}, bf16[576,640]{1,0:T(8,128)(2,1)}, u32[]{:S(2)}) copy-start(bf16[576,640]{1,0:T(8,128)(2,1)} %constant.66.clone.low_ref) | copy-start | bytes 2211844
  30.6 94.5 %copy-start.10 = (s32[144,256]{1,0:T(8,128)S(1)}, s32[144,256]{1,0:T(8,128)}, u32[]{:S(2)}) copy-start(s32[144,256]{1,0:T(8,128)} %height_ref.3) | copy-start | bytes 442372
  49.4 0.9 copy-start.11
  103.4 21.6 %all-to-all-start.1 = ((f32[8,80,256]{2,1,0:T(8,128)}), f32[8,80,256]{2,1,0:T(8,128)S(1)}, u32[]{:S(2)}, u32[]{:S(2)}) async-start(f32[8,80,256]{2,1,0:T(8,128)} %get-tuple-element.8), calls=%async_computation.1 | async-start | bytes 1310720 | tf_op jit(solution)/shard_map/all_to_all | solution.py:421
  125.0 2.3 %copy-start.1 = (f32[2,16,144,256]{3,2,1,0:T(8,128)S(1)}, f32[2,16,144,256]{3,2,1,0:T(8,128)}, u32[]{:S(2)}) copy-start(f32[2,16,144,256]{3,2,1,0:T(8,128)} %projector_ref.3) | copy-start | bytes 14155780
  127.4 1.3 copy-start.4
Sparse Core Ops, SparseCore 0:
  32.5 29.1 all-gather.1

commit v3 on v2

--- a/solution.py
+++ b/solution.py
@@ -66,6 +66,43 @@
     return dot(table_high, high) + dot(table_low, high) + dot(table_high, low)
 
 
+def fft_peer(i, count):
+    return lax.axis_index("band"), lax.rem(lax.axis_index("fft") + i, count)
+
+
+def band_peer(i, count):
+    return lax.rem(lax.axis_index("band") + i, count), lax.axis_index("fft")
+
+
+def greet(peer, count):
+    barrier = pltpu.get_barrier_semaphore()
+    for i in range(1, count):
+        pl.semaphore_signal(barrier, inc=1, device_id=peer(i, count), device_id_type=MESH)
+
+
+def exchange(peer, count, source, slots, send, receive):
+    copies = []
+    for i in range(1, count):
+        copy = pltpu.make_async_remote_copy(
+            src_ref=source(i),
+            dst_ref=slots.at[i],
+            send_sem=send.at[i],
+            recv_sem=receive.at[i],
+            device_id=peer(i, count),
+            device_id_type=MESH,
+        )
+        copy.start()
+        copies.append(copy)
+    return copies
+
+
+def swap_blocks(count, blocks, slots, send, receive):
+    fft = lax.axis_index("fft")
+    return exchange(
+        fft_peer, count, lambda i: blocks.at[lax.rem(fft + i, count)], slots, send, receive
+    )
+
+
 def fold(row):
     return sum(row[:, i : i + LANES] for i in range(0, row.shape[1], LANES))
 
@@ -77,7 +114,11 @@
     high_ref,
     low_ref,
     projector_ref,
+    landed_ref,
     out_ref,
+    slots_in,
+    send,
+    receive,
     dense,
     slot_heights,
     slot_values,
@@ -89,6 +130,7 @@
     projector_count = projector_ref.shape[1]
     fetch = pltpu.make_async_copy(projector_ref, held, arrived)
     fetch.start()
+    greet(fft_peer, landed_ref.shape[0])
     block = NZ // 2
     base = lax.broadcasted_iota(jnp.int32, (block, LANES), 0)
     for lane in range(0, sticks, LANES):
@@ -131,6 +173,13 @@
     sums = jnp.broadcast_to(sums, (8, sticks))
     for device in range(devices):
         out_ref[device, 2 * padded :, :] = sums
+    pl.semaphore_wait(pltpu.get_barrier_semaphore(), devices - 1)
+    copies = swap_blocks(devices, out_ref, slots_in, send, receive)
+    fft = lax.axis_index("fft")
+    landed_ref[fft] = out_ref[fft]
+    for i, copy in enumerate(copies, 1):
+        copy.wait()
+        landed_ref[lax.rem(fft - i + devices, devices)] = slots_in[i]
 
 
 def plane_kernel(
@@ -232,43 +281,53 @@
 
 def final_kernel(
     weight_ref,
-    back_ref,
+    value_ref,
     high_ref,
     low_ref,
     height_ref,
     plane_kinetic_ref,
     orbital_ref,
+    projector_any,
+    all_any,
+    out_ref,
+    column_ref,
     projector_ref,
     all_ref,
-    out_ref,
+    fetched,
+    slots_in,
+    back_ref,
+    send,
+    receive,
     sum_ref,
+    own,
+    summed,
+    fft_in,
+    band_in,
+    fft_send,
+    fft_receive,
+    band_send,
+    band_receive,
     spectrum,
 ):
     devices, double, sticks = back_ref.shape
+    band_count = column_ref.shape[0]
+    first_fetch = pltpu.make_async_copy(projector_any, projector_ref, fetched.at[0])
+    second_fetch = pltpu.make_async_copy(all_any, all_ref, fetched.at[1])
+    first_fetch.start()
+    second_fetch.start()
+    greet(fft_peer, devices)
+    greet(band_peer, band_count)
+    pl.semaphore_wait(pltpu.get_barrier_semaphore(), devices + band_count - 2)
+    copies = swap_blocks(devices, value_ref, slots_in, send, receive)
+    fft, mine = lax.axis_index("fft"), lax.axis_index("band")
+    back_ref[fft] = value_ref[fft]
+    first_fetch.wait()
+    second_fetch.wait()
     padded = double // 2
     slots = height_ref.shape[0]
     projector_count = projector_ref.shape[1]
     band_total = all_ref.shape[1]
     grid_total = NX * NY * NZ
-    back = back_ref[...].reshape(devices * 2 * padded, sticks)
-    result = dot3(high_ref[...], low_ref[...], back)
-    for lane in range(0, sticks, LANES):
-        spectrum[lane // LANES] = result[:, lane : lane + LANES]
-    for lane in range(0, sticks, LANES):
-        lanes = slice(lane, lane + LANES)
-        heights = height_ref[:, lanes]
-
-        def step(height, carry):
-            real, imag = carry
-            here = heights == height
-            row_r = spectrum[lane // LANES, pl.ds(height, 1), :]
-            row_i = spectrum[lane // LANES, pl.ds(NZ + height, 1), :]
-            return jnp.where(here, row_r, real), jnp.where(here, row_i, imag)
-
-        zero = jnp.zeros((slots, LANES), F32)
-        real, imag = lax.fori_loop(0, NZ, step, (zero, zero), unroll=4)
-        out_ref[0, 0, :, lanes] = real / grid_total
-        out_ref[1, 0, :, lanes] = imag / grid_total
     row_count = 48
     for first in range(0, slots, row_count):
         at = slice(first, first + row_count)
@@ -285,71 +344,57 @@
                 real = real + (pr * wr - pi * wi)
                 imag = imag + (pr * wi + pi * wr)
             out_ref[0, 0, at, lanes] = (
-                kinetic * orbital_ref[0, 0, at, lanes] + out_ref[0, 0, at, lanes] + real
+                kinetic * orbital_ref[0, 0, at, lanes] + real
             )
             out_ref[1, 0, at, lanes] = (
-                kinetic * orbital_ref[1, 0, at, lanes] + out_ref[1, 0, at, lanes] + imag
+                kinetic * orbital_ref[1, 0, at, lanes] + imag
             )
+    for i, copy in enumerate(copies, 1):
+        copy.wait()
+        back_ref[lax.rem(fft - i + devices, devices)] = slots_in[i]
+    back = back_ref[...].reshape(devices * 2 * padded, sticks)
+    result = dot3(high_ref[...], low_ref[...], back)
+    for lane in range(0, sticks, LANES):
+        spectrum[lane // LANES] = result[:, lane : lane + LANES]
+    for lane in range(0, sticks, LANES):
+        lanes = slice(lane, lane + LANES)
+        heights = height_ref[:, lanes]
+
+        def step(height, carry):
+            real, imag = carry
+            here = heights == height
+            row_r = spectrum[lane // LANES, pl.ds(height, 1), :]
+            row_i = spectrum[lane // LANES, pl.ds(NZ + height, 1), :]
+            return jnp.where(here, row_r, real), jnp.where(here, row_i, imag)
+
+        zero = jnp.zeros((slots, LANES), F32)
+        real, imag = lax.fori_loop(0, NZ, step, (zero, zero), unroll=4)
+        out_ref[0, 0, :, lanes] = out_ref[0, 0, :, lanes] + real / grid_total
+        out_ref[1, 0, :, lanes] = out_ref[1, 0, :, lanes] + imag / grid_total
     for band in range(band_total):
         hr, hi = out_ref[0, 0], out_ref[1, 0]
         br, bi = all_ref[0, band], all_ref[1, band]
-        sum_ref[0, band : band + 1, :] = jnp.sum(br * hr + bi * hi, axis=0, keepdims=True)
-        sum_ref[1, band : band + 1, :] = jnp.sum(br * hi - bi * hr, axis=0, keepdims=True)
-
-
-def gather_kernel(
-    fft_count, band_count, sum_ref, out_ref, own, summed, fft_in, band_in, fs, fr, bs, br
-):
-    fft, band = lax.axis_index("fft"), lax.axis_index("band")
-    barrier = pltpu.get_barrier_semaphore()
-    for i in range(1, fft_count):
-        pl.semaphore_signal(
-            barrier, inc=1, device_id=(band, lax.rem(fft + i, fft_count)), device_id_type=MESH
-        )
-    for i in range(1, band_count):
-        pl.semaphore_signal(
-            barrier, inc=1, device_id=(lax.rem(band + i, band_count), fft), device_id_type=MESH
-        )
+        sum_ref[band : band + 1, :] = jnp.sum(br * hr + bi * hi, axis=0, keepdims=True)
+        sum_ref[band_total + band : band_total + band + 1, :] = jnp.sum(br * hi - bi * hr, axis=0, keepdims=True)
     own[...] = fold(sum_ref[...])
-    pl.semaphore_wait(barrier, fft_count + band_count - 2)
-
-    def exchange(count, source, slots, send, receive, target):
-        copies = []
-        for i in range(1, count):
-            copy = pltpu.make_async_remote_copy(
-                src_ref=source,
-                dst_ref=slots.at[i],
-                send_sem=send.at[i],
-                recv_sem=receive.at[i],
-                device_id=target(i),
-                device_id_type=MESH,
-            )
-            copy.start()
-            copies.append(copy)
-        return copies
-
-    copies = exchange(
-        fft_count, own, fft_in, fs, fr, lambda i: (band, lax.rem(fft + i, fft_count))
-    )
-    for copy in copies:
+    for copy in exchange(fft_peer, devices, lambda i: own, fft_in, fft_send, fft_receive):
         copy.wait()
     fft_in[0] = own[...]
     total = jnp.zeros_like(own)
-    for i in range(fft_count):
-        total = total + fft_in[lax.rem(fft - i + fft_count, fft_count)]
+    for i in range(devices):
+        total = total + fft_in[lax.rem(fft - i + devices, devices)]
     summed[...] = total
-    copies = exchange(
-        band_count, summed, band_in, bs, br, lambda i: (lax.rem(band + i, band_count), fft)
-    )
-    for copy in copies:
+    for copy in exchange(band_peer, band_count, lambda i: summed, band_in, band_send, band_receive):
         copy.wait()
     band_in[0] = summed[...]
     for i in range(band_count):
-        out_ref[i] = band_in[lax.rem(band - i + band_count, band_count)]
-
-
-def params(mebibytes):
-    return pltpu.CompilerParams(vmem_limit_bytes=mebibytes << 20)
+        column_ref[i] = band_in[lax.rem(mine - i + band_count, band_count)]
+
+
+def params(mebibytes, number=None):
+    return pltpu.CompilerParams(
+        vmem_limit_bytes=mebibytes << 20, collective_id=number, has_side_effects=number is not None
+    )
 
 
 def body(orbitals, potential, projectors, coupling, stick_column, stick_heights, projector_atom):
@@ -378,12 +423,16 @@
     forth = (devices, 2 * padded + 8, sticks_here)
     back = (devices, 2 * padded, sticks_here)
     anywhere = pl.BlockSpec(memory_space=pl.ANY)
-    z_space = pl.pallas_call(
+    received = pl.pallas_call(
         functools.partial(normal_kernel, planes_here),
         in_specs=[vmem] * 4 + [anywhere],
         out_specs=vmem,
         out_shape=jax.ShapeDtypeStruct(forth, F32),
         scratch_shapes=[
+            pltpu.VMEM(forth, F32),
+            pltpu.VMEM(forth, F32),
+            pltpu.SemaphoreType.DMA((devices,)),
+            pltpu.SemaphoreType.DMA((devices,)),
             pltpu.VMEM((2 * NZ, sticks_here), F32),
             pltpu.VMEM((slot_count, LANES), jnp.int32),
             pltpu.VMEM((2, slot_count, LANES), F32),
@@ -391,10 +440,9 @@
             pltpu.VMEM((LANES, LANES), F32),
             pltpu.SemaphoreType.DMA,
         ],
-        compiler_params=params(24),
+        compiler_params=params(56, 0),
         cost_estimate=pl.CostEstimate(flops=600000000, bytes_accessed=3000000, transcendentals=0),
     )(orbitals, stick_heights, z_high, z_low, projectors)
-    received = lax.all_to_all(z_space, "fft", split_axis=0, concat_axis=0, tiled=True)
     values, total = pl.pallas_call(
         plane_kernel,
         in_specs=[smem] + [vmem] * 3,
@@ -418,23 +466,40 @@
     same_atom = projector_atom[:, None] == projector_atom[None, :]
     atom_coupling = jnp.where(same_atom, 0.5 * (coupling + coupling.T), jnp.zeros_like(coupling))
     weighted = jnp.einsum("kl,plb->pkb", atom_coupling, projections, precision=HIGHEST)
-    results = lax.all_to_all(values, "fft", split_axis=0, concat_axis=0, tiled=True)
-    applied_h, sums = pl.pallas_call(
+    band_devices = band_total // orbitals.shape[1]
+    rows = 2 * band_total
+    applied_h, gathered = pl.pallas_call(
         final_kernel,
-        in_specs=[smem] + [vmem] * 8,
+        in_specs=[smem] + [vmem] * 6 + [anywhere] * 2,
         out_specs=(vmem, vmem),
         out_shape=(
             jax.ShapeDtypeStruct(orbitals.shape, F32),
-            jax.ShapeDtypeStruct((2, band_total, sticks_here), F32),
+            jax.ShapeDtypeStruct((band_devices, rows, LANES), F32),
         ),
         scratch_shapes=[
+            pltpu.VMEM(projectors.shape, F32),
+            pltpu.VMEM(all_orbitals.shape, F32),
+            pltpu.SemaphoreType.DMA((2,)),
+            pltpu.VMEM(back, F32),
+            pltpu.VMEM(back, F32),
+            pltpu.SemaphoreType.DMA((devices,)),
+            pltpu.SemaphoreType.DMA((devices,)),
+            pltpu.VMEM((rows, sticks_here), F32),
+            pltpu.VMEM((rows, LANES), F32),
+            pltpu.VMEM((rows, LANES), F32),
+            pltpu.VMEM((devices, rows, LANES), F32),
+            pltpu.VMEM((band_devices, rows, LANES), F32),
+            pltpu.SemaphoreType.DMA((devices,)),
+            pltpu.SemaphoreType.DMA((devices,)),
+            pltpu.SemaphoreType.DMA((band_devices,)),
+            pltpu.SemaphoreType.DMA((band_devices,)),
             pltpu.VMEM((sticks_here // LANES, 2 * NZ, LANES), F32),
         ],
-        compiler_params=params(40),
+        compiler_params=params(56, 1),
         cost_estimate=pl.CostEstimate(flops=600000000, bytes_accessed=9000000, transcendentals=0),
     )(
         weighted[:, :, 0] * norm_scale,
-        results,
+        values,
         back_high,
         back_low,
         stick_heights,
@@ -443,25 +508,6 @@
         projectors,
         all_orbitals,
     )
-    band_devices = band_total // orbitals.shape[1]
-    rows = 2 * band_total
-    gathered = pl.pallas_call(
-        functools.partial(gather_kernel, devices, band_devices),
-        in_specs=[vmem],
-        out_specs=vmem,
-        out_shape=jax.ShapeDtypeStruct((band_devices, rows, LANES), F32),
-        scratch_shapes=[
-            pltpu.VMEM((rows, LANES), F32),
-            pltpu.VMEM((rows, LANES), F32),
-            pltpu.VMEM((devices, rows, LANES), F32),
-            pltpu.VMEM((band_devices, rows, LANES), F32),
-            pltpu.SemaphoreType.DMA((devices,)),
-            pltpu.SemaphoreType.DMA((devices,)),
-            pltpu.SemaphoreType.DMA((band_devices,)),
-            pltpu.SemaphoreType.DMA((band_devices,)),
-        ],
-        compiler_params=pltpu.CompilerParams(collective_id=0, has_side_effects=True),
-    )(sums.reshape(rows, sticks_here))
     subspace = jnp.sum(gathered, axis=2).reshape(band_devices, 2, band_total)
     subspace = jnp.transpose(subspace, (1, 2, 0)) / coeff_total
     return (applied_h, projections, subspace)

time: 158 us -> 140 us (0.89)
  Pallas kernels: 82.7 us -> 118 us
  waiting for transfers between devices: 35.1 us -> 0.68 us
  starting transfers between devices: 9.91 us -> 0.04 us
  local copies, waits for them, and re-layouts: 13.2 us -> 3.34 us
    all_to_all x2 -> x0, waiting for transfers between devices: 34.4 us -> none  [the longest x1 18.8 us: body(): lax.all_to_all(z_space, 'fft', split_axis=0, concat_axis=0, tiled=True)]
    pallas_call x2 -> x1, Pallas kernels: 19.8 us -> 38.4 us  [body(): pl.pallas_call(final_kernel, in_specs=[smem] + [vmem] * 6 + [anywhere] *...]
    pallas_call x1, Pallas kernels: 9.77 us -> 26.5 us  [body(): pl.pallas_call(functools.partial(normal_kernel, planes_here), in_specs=[v...]
    all_to_all x2 -> x0, starting transfers between devices: 9.88 us -> none  [the longest x1 6.34 us: body(): lax.all_to_all(z_space, 'fft', split_axis=0, concat_axis=0, tiled=True)]
    unnamed x30 -> x7, local copies, waits for them, and re-layouts: 11.8 us -> 2.46 us
  transfers between devices with their start and end apart: 3 -> 1, of which waited for: 2 -> 0; matrix products, arithmetic and copies ran while one was open for 2% -> 3% of each run, Pallas kernels for 34% -> 57%
where the time goes in v3:
time: 140 us
  Pallas kernels  118 us (84%)
  between operations  14.1 us (10%)
  local copies, waits for them, and re-layouts  3.34 us (2%)
  other arithmetic  2.71 us (2%)
    pallas_call x1, Pallas kernels, body(): pl.pallas_call(plane_kernel, in_specs=[smem] + [vmem] * 3, out_specs=(vme...  53.1 us
    pallas_call x1, Pallas kernels, body(): pl.pallas_call(final_kernel, in_specs=[smem] + [vmem] * 6 + [anywhere] *...  38.4 us
    pallas_call x1, Pallas kernels, body(): pl.pallas_call(functools.partial(normal_kernel, planes_here), in_specs=[v...  26.5 us
  transfers between devices with their start and end apart: 1, of which 0 were waited for; matrix products, arithmetic and copies ran while one was open for 3% of the time, Pallas kernels for 57%

profile of v3, /device:TPU:0, one launch (start us, length us, event | category | flops | bytes accessed | tf_op | source)
XLA Modules:
  0.0 139.6 jit_solution(2314568504651089149)
XLA Ops:
  7.2 0.0 all-gather.2.cloned.1.call-start
  7.2 0.7 all-gather.2.cloned.1.call-update
  7.9 26.5 %shard_map.139.received_ref = f32[8,88,256]{2,1,0:T(8,128)} custom-call(f32[2,1,144,256]{3,2,1,0:T(8,128)} %orbital_ref.3, s32[144,256]{1,0:T(8,128)} %height_ref.3, bf16[640,576]{1,0:T(8,128)(2,1)} %constant.62.clone.high_ref, bf16[640,576]{1,0:T(8,128)(2,1)} %constant.63.clone.low_ref, f32[2,16,144,256]{3,2,1,0:T(8,128)} %projector_any.1), custom_call_target="tpu_custom_call" | custom-call | flops 600000000 | bytes 3000000 | tf_op jit(solution)/shard_map/pallas_call | solution.py:426
  34.4 0.0 copy-start
  34.4 0.0 copy-start.1
  34.5 53.1 %shard_map.140 = (f32[8,80,256]{2,1,0:T(8,128)}, f32[8,128]{1,0:T(8,128)}) custom-call(s32[2048]{0:T(1024)} %column_ref.1, f32[8,88,256]{2,1,0:T(8,128)} %shard_map.139.received_ref, f32[36,20736]{1,0:T(8,128)} %potential_ref.1, bf16[288,432]{1,0:T(8,128)(2,1)} %constant.64.clone.table_ref), custom_call_target="tpu_custom_call" | custom-call | flops 60000002048 | bytes 6000000 | tf_op jit(solution)/shard_map/pallas_call | solution.py:446
  87.6 0.7 slice_reduce_fusion
  88.3 0.1 reshape_squeeze.3
  88.4 0.0 copy-done
  88.4 0.1 copy.15
  88.5 1.3 fusion.12
  89.8 0.6 slice_multiply_fusion
  90.4 0.0 copy-done.1
  90.4 0.8 convolution_multiply_fusion.weight_ref
  91.1 0.0 all-gather.2.cloned.1.call-done.all_any
  91.1 38.4 %shard_map.141 = (f32[2,1,144,256]{3,2,1,0:T(8,128)}, f32[4,8,128]{2,1,0:T(8,128)}) custom-call(f32[2,16]{1,0:T(2,128)} %convolution_multiply_fusion.weight_ref, f32[8,80,256]{2,1,0:T(8,128)} %get-tuple-element.8.value_ref, bf16[576,640]{1,0:T(8,128)(2,1)} %constant.65.clone.high_ref, bf16[576,640]{1,0:T(8,128)(2,1)} %constant.66.clone.low_ref, ...), custom_call_target="tpu_custom_call" | custom-call | flops 600000000 | bytes 9000000 | tf_op jit(solution)/shard_map/pallas_call | solution.py:471
  129.5 0.8 reduce_sum.9
  130.3 0.1 div.27
  130.4 0.7 copy.17
  131.1 1.7 %copy.19 = f32[2,1,144,256]{3,2,1,0:T(8,128)} copy(f32[2,1,144,256]{3,2,1,0:T(8,128)} %get-tuple-element.17) | data formatting | bytes 589824
  (1 shorter events, 0.0 us)
Async XLA Ops:
  7.2 84.0 %all-gather.2.cloned.1.call-start = ((), (), s32[]{:S(2)}) async-start(), calls=%async_computation | async-start | bytes 1474560 | tf_op jit(solution)/shard_map/all_gather | solution.py:415
  34.4 54.0 %copy-start = (f32[16,16]{1,0:T(8,128)S(1)}, f32[16,16]{1,0:T(8,128)}, u32[]{:S(2)}) copy-start(f32[16,16]{1,0:T(8,128)} %param.15) | copy-start | bytes 3076
  34.4 55.9 %copy-start.1 = (s32[16]{0:T(128)S(1)}, s32[16]{0:T(128)}, u32[]{:S(2)}) copy-start(s32[16]{0:T(128)} %param.18) | copy-start | bytes 196
Sparse Core Ops, SparseCore 0:
  9.8 30.4 all-gather.1
